TPU v7x, 32 devices: a whole 2x2x4 slice. The times are simulated.
32 devices in a mesh: row: 16 (over z, x, core), col: 2 (over y).
Axes of the slice: x: 2, y: 2, z: 4, core: 2. Of those that a mesh axis runs over, the one named last changes fastest.
Arguments:
- right_sides: float32 [8192, 1024], P('row', 'col'), may hold values from -6 to 6
- pencil_s: float32 [8192, 512], P('row'), as said below
- pencil_t: float32 [8192, 512], P('row'), as said below
- value_alpha: float32 [4096], replicated, may hold values from -3 to -0.5
- value_beta: float32 [4096], replicated, may hold values from 0.5 to 1
- selected: int32 [1024], P('col'), may hold values from 0 to 4095
- block_slot: int32 [32], replicated, may hold values from 0 to 31, as said below
- right_basis: float32 [65536, 2, 256], P('row', None, 'col'), may hold values from -0.25 to 0.25
- vectors: float32 [65536, 1024], P('row', 'col'), may hold values from -6 to 6
Outputs:
- updated_sides: float32 [8192, 1024], P('row', 'col')
- updated_vectors: float32 [65536, 1024], P('row', 'col')
Inputs may be any that keep to these rules, and one draw needn't show every extreme that they name: A permutation: logical block b of 256 rows is stored at slot block_slot[b]. `pencil_s`: in the window, entries left of the diagonal are 0 and diagonal entries lie in [1, 2]. `pencil_t`: in the window, entries left of the diagonal are 0 and diagonal entries lie in [1, 2].
All inputs are finite; a program needn't handle non-finite values.
Results may differ from a plain program's by a relative error of at most 0.0003.
Values sent between devices are 32-bit elements; how exact they have to be, the bound alone decides.
No kernel may reach another device: no remote copies, remote signals or barrier semaphores. Data moves between devices by JAX's collectives and lax.ppermute only.
A program may use at most 128 MiB of HBM per device.

v0:
```python
import functools
import math

import jax
import jax.numpy as jnp
from jax import lax
from jax.experimental import pallas as pl
from jax.experimental.pallas import tpu as pltpu
from jax.sharding import PartitionSpec as P

SUB = 32
GROUP = 8
VMEM_BYTES = 57 * 1024 * 1024
ADD_VMEM_BYTES = 48 * 1024 * 1024
FULL_VMEM_BYTES = 59 * 1024 * 1024
TILE = 512
LIGHT = pl.CostEstimate(flops=1000, bytes_accessed=1000, transcendentals=0)


def exact_dot(left, right):
    return jnp.dot(left, right, precision=lax.Precision.HIGHEST, preferred_element_type=jnp.float32)


def split_two(value):
    high = value.astype(jnp.bfloat16)
    low = (value - high.astype(jnp.float32)).astype(jnp.bfloat16)
    return high, low


def split_three(value):
    high = value.astype(jnp.bfloat16)
    rest = value - high.astype(jnp.float32)
    middle = rest.astype(jnp.bfloat16)
    low = (rest - middle.astype(jnp.float32)).astype(jnp.bfloat16)
    return high, middle, low


def stacked_dot(left, right):
    high, middle, low = split_three(left)
    top, mid, end = split_three(right)
    return jnp.dot(
        jnp.concatenate([high, middle, high, middle, high, low], axis=1),
        jnp.concatenate([top, top, mid, mid, end, top], axis=0),
        preferred_element_type=jnp.float32,
    )


def table_lookup(selected, table):
    table_rows, lanes = table.shape
    lane = lax.broadcasted_iota(jnp.int32, (lanes, selected.shape[1]), 0)
    in_lane = jnp.where(lane == selected % lanes, 1.0, 0.0)
    candidates = exact_dot(table, in_lane)
    row = lax.broadcasted_iota(jnp.int32, candidates.shape, 0)
    return jnp.sum(jnp.where(row == selected // lanes, candidates, 0.0), axis=0, keepdims=True)


def back_substitute(s_ref, t_ref, alpha, beta, pending_ref, x_ref):
    size = x_ref.shape[0]
    rows = lax.broadcasted_iota(jnp.int32, (SUB, SUB), 0)
    cols = lax.broadcasted_iota(jnp.int32, (SUB, SUB), 1)
    groups = SUB // GROUP
    for first in range(size - SUB, -1, -SUB):
        s_small = s_ref[first : first + SUB, first : first + SUB]
        t_small = t_ref[first : first + SUB, first : first + SUB]
        s_diag = jnp.sum(jnp.where(rows == cols, s_small, 0.0), axis=1, keepdims=True)
        t_diag = jnp.sum(jnp.where(rows == cols, t_small, 0.0), axis=1, keepdims=True)
        inverse = 1.0 / (beta * s_diag - alpha * t_diag)
        s_strict = jnp.where(rows < cols, s_small, 0.0)
        t_strict = jnp.where(rows < cols, t_small, 0.0)
        pending = [
            pending_ref[first + g * GROUP : first + (g + 1) * GROUP, :] for g in range(groups)
        ]
        for column in range(SUB - 1, -1, -1):
            own, row = divmod(column, GROUP)
            right = pending[own][row : row + 1, :]
            reciprocal = inverse[column : column + 1, :]
            x_ref[first + column : first + column + 1, :] = right * reciprocal
            scaled_beta = beta * reciprocal
            scaled_alpha = alpha * reciprocal
            for g in range(own + 1):
                span = slice(g * GROUP, (g + 1) * GROUP)
                factor = (
                    s_strict[span, column : column + 1] * scaled_beta
                    - t_strict[span, column : column + 1] * scaled_alpha
                )
                pending[g] = pending[g] - factor * right
        if first:
            block = x_ref[first : first + SUB, :]
            columns = slice(first, first + SUB)
            pending_ref[:first, :] = pending_ref[:first, :] - stacked_dot(
                jnp.concatenate([s_ref[:first, columns], t_ref[:first, columns]], axis=1),
                jnp.concatenate([beta * block, -alpha * block], axis=0),
            )


def put_together(core, side, piece_refs, whole_ref):
    quarter = whole_ref.shape[0] // 4
    places = [(core, side), (core, 1 - side), (1 - core, side), (1 - core, 1 - side)]
    for ref, (half, part) in zip(piece_refs, places):
        start = (2 * half + part) * quarter
        whole_ref[pl.ds(pl.multiple_of(start, quarter), quarter), :] = ref[...]


def hand_out(core, x_ref, kept_ref, given_ref):
    half = kept_ref.shape[0]
    kept_ref[...] = x_ref[pl.ds(pl.multiple_of(core * half, half), half), :]
    given_ref[...] = x_ref[pl.ds(pl.multiple_of((1 - core) * half, half), half), :]


def lower_kernel(
    slots, me, s_ref, t_ref, r_ref, values_a, values_b, selected, kept_ref, given_ref, *refs
):
    alpha_ref, beta_ref, pending_ref, x_ref = refs
    alpha = table_lookup(selected[...], values_a[...])
    beta = table_lookup(selected[...], values_b[...])
    alpha_ref[...] = alpha
    beta_ref[...] = beta
    pending_ref[...] = r_ref[...]
    back_substitute(s_ref, t_ref, alpha, beta, pending_ref, x_ref)
    hand_out(me[0] & 1, x_ref, kept_ref, given_ref)


def upper_kernel(slots, me, s_ref, t_ref, r_ref, alpha_ref, beta_ref, *refs):
    piece_refs, (kept_ref, given_ref, lower_ref, pending_ref, x_ref) = refs[:4], refs[4:]
    block = x_ref.shape[0]
    alpha, beta = alpha_ref[...], beta_ref[...]
    put_together(me[0] & 1, (me[0] >> 1) & 1, piece_refs, lower_ref)
    lower = lower_ref[...]
    pending_ref[...] = r_ref[...] - (
        exact_dot(s_ref[:, block:], beta * lower) - exact_dot(t_ref[:, block:], alpha * lower)
    )
    back_substitute(s_ref, t_ref, alpha, beta, pending_ref, x_ref)
    hand_out(me[0] & 1, x_ref, kept_ref, given_ref)


def solve_lower(slots, me, pencil_s, pencil_t, sides, value_alpha, value_beta, selected):
    block, eigs = pencil_s.shape[1] // 2, sides.shape[1]
    count, last = sides.shape[0] // block, slots.shape[0] - 1
    lanes = 128 if value_alpha.shape[0] % 128 == 0 else value_alpha.shape[0]
    table_shape = (value_alpha.shape[0] // lanes, lanes)
    corner = pl.BlockSpec((block, block), lambda i, slots, me: (lax.rem(slots[last], count), 1))
    whole = pl.BlockSpec((block, eigs), lambda i, slots, me: (lax.rem(slots[last], count), 0))
    line = pl.BlockSpec((1, eigs), lambda i, slots, me: (0, 0))
    half = pl.BlockSpec((block // 2, eigs), lambda i, slots, me: (0, 0))
    table = pl.BlockSpec(table_shape, lambda i, slots, me: (0, 0))
    return pl.pallas_call(
        lower_kernel,
        out_shape=(
            *[jax.ShapeDtypeStruct((block // 2, eigs), jnp.float32)] * 2,
            jax.ShapeDtypeStruct((1, eigs), jnp.float32),
            jax.ShapeDtypeStruct((1, eigs), jnp.float32),
        ),
        grid_spec=pltpu.PrefetchScalarGridSpec(
            num_scalar_prefetch=2,
            grid=(1,),
            in_specs=[corner, corner, whole, table, table, line],
            out_specs=(*[half] * 2, line, line),
            scratch_shapes=[pltpu.VMEM((block, eigs), jnp.float32)] * 2,
        ),
        compiler_params=pltpu.CompilerParams(vmem_limit_bytes=FULL_VMEM_BYTES),
        cost_estimate=LIGHT,
        name="solve_lower",
    )(
        slots,
        me,
        pencil_s,
        pencil_t,
        sides,
        value_alpha.reshape(table_shape),
        value_beta.reshape(table_shape),
        selected[None, :],
    )


def solve_upper(slots, me, pencil_s, pencil_t, sides, alpha, beta, pieces):
    block, eigs = pencil_s.shape[1] // 2, sides.shape[1]
    count, index = sides.shape[0] // block, slots.shape[0] - 2
    band = pl.BlockSpec((block, 2 * block), lambda i, slots, me: (lax.rem(slots[index], count), 0))
    whole = pl.BlockSpec((block, eigs), lambda i, slots, me: (lax.rem(slots[index], count), 0))
    line = pl.BlockSpec((1, eigs), lambda i, slots, me: (0, 0))
    fixed = [pl.BlockSpec(piece.shape, lambda i, slots, me: (0, 0)) for piece in pieces]
    return pl.pallas_call(
        upper_kernel,
        out_shape=(
            *[jax.ShapeDtypeStruct((block // 2, eigs), jnp.float32)] * 2,
            jax.ShapeDtypeStruct((block, eigs), jnp.float32),
        ),
        grid_spec=pltpu.PrefetchScalarGridSpec(
            num_scalar_prefetch=2,
            grid=(1,),
            in_specs=[band, band, whole, line, line, *fixed],
            out_specs=(
                *[pl.BlockSpec((block // 2, eigs), lambda i, slots, me: (0, 0))] * 2,
                pl.BlockSpec((block, eigs), lambda i, slots, me: (0, 0)),
            ),
            scratch_shapes=[pltpu.VMEM((block, eigs), jnp.float32)] * 2,
        ),
        compiler_params=pltpu.CompilerParams(vmem_limit_bytes=FULL_VMEM_BYTES),
        cost_estimate=LIGHT,
        name="solve_upper",
    )(slots, me, pencil_s, pencil_t, sides, alpha, beta, *pieces)


def near_dot(left, right_terms):
    high, low = split_two(left)
    return jnp.dot(
        jnp.concatenate([high, low, high], axis=1), right_terms, preferred_element_type=jnp.float32
    )


def three_terms(right):
    high, low = split_two(right)
    return jnp.concatenate([high, high, low], axis=0)


def finish_kernel(slots, me, parts, r_ref, s_ref, t_ref, alpha_ref, beta_ref, lower_ref, *refs):
    piece_refs, (out_ref, terms_ref, upper_ref) = refs[:4], refs[4:]
    put_together(me[0] & 1, (me[0] >> 1) & 1, piece_refs, upper_ref)
    block = upper_ref.shape[0]
    width = block // parts.shape[0]
    for part in range(parts.shape[0]):
        rows = pl.ds(pl.multiple_of(parts[part] * width, width), width)
        for half, source in enumerate((upper_ref, lower_ref)):
            target = (2 * part + half) * width
            high, low = split_two(source[rows, :])
            for term, value in enumerate((high, high, low)):
                first = 2 * block * term + target
                terms_ref[first : first + width, :] = value
    count = out_ref.shape[0] // block
    base = me[0] * count
    alpha, beta = alpha_ref[...], beta_ref[...]
    upper, lower = upper_ref[...], lower_ref[...]
    x = jnp.concatenate([upper, lower], axis=0)
    update = near_dot(s_ref[...], three_terms(beta * x)) - near_dot(t_ref[...], three_terms(alpha * x))
    for slot in range(count):
        span = slice(slot * block, (slot + 1) * block)
        fresh = r_ref[span, :] - update[span, :]
        fresh = jnp.where(slots[slots.shape[0] - 2] == base + slot, upper, fresh)
        out_ref[span, :] = jnp.where(slots[slots.shape[0] - 1] == base + slot, lower, fresh)


def finish_sides(slots, me, parts, sides, pencil_s, pencil_t, alpha, beta, lower, pieces):
    block, eigs = lower.shape
    smem, vmem = pl.BlockSpec(memory_space=pltpu.SMEM), pl.BlockSpec(memory_space=pltpu.VMEM)
    return pl.pallas_call(
        finish_kernel,
        out_shape=(
            jax.ShapeDtypeStruct(sides.shape, jnp.float32),
            jax.ShapeDtypeStruct((6 * block, eigs), jnp.bfloat16),
        ),
        in_specs=[smem] * 3 + [vmem] * (6 + len(pieces)),
        out_specs=(vmem, vmem),
        scratch_shapes=[pltpu.VMEM((block, eigs), jnp.float32)],
        compiler_params=pltpu.CompilerParams(vmem_limit_bytes=VMEM_BYTES),
        cost_estimate=LIGHT,
        name="finish_sides",
    )(slots, me, parts, sides, pencil_s, pencil_t, alpha, beta, lower, *pieces)


def add_kernel(paired, base_ref, terms_ref, *refs):
    part_refs, out_ref = refs[: len(refs) - 1], refs[-1]
    tile = out_ref.shape[0]
    pieces = []
    for ref in part_refs:
        if paired:
            pieces.append(ref[pl.ds(0, tile, 2), :])
            pieces.append(ref[pl.ds(1, tile, 2), :])
        else:
            pieces.append(ref[...])
    basis = jnp.concatenate(pieces, axis=1)
    out_ref[...] = base_ref[...] + near_dot(basis, terms_ref[...])


def add_product(vectors, terms, parts, paired):
    rows, eigs = vectors.shape
    tile = math.gcd(TILE, rows)
    per, width = parts[0].shape[0] // rows, parts[0].shape[1]

    def stream(height, lanes):
        return pl.BlockSpec((height, lanes), lambda i: (i, 0))

    return pl.pallas_call(
        functools.partial(add_kernel, paired),
        out_shape=jax.ShapeDtypeStruct((rows, eigs), jnp.float32),
        grid=(rows // tile,),
        in_specs=[stream(tile, eigs), pl.BlockSpec(memory_space=pltpu.VMEM)]
        + [stream(per * tile, width) for _ in parts],
        out_specs=pl.BlockSpec((tile, eigs), lambda i: (i, 0)),
        compiler_params=pltpu.CompilerParams(vmem_limit_bytes=ADD_VMEM_BYTES),
        cost_estimate=LIGHT,
        name="add_product",
    )(vectors, terms, *parts)


def spread(kept, given, me, owner, axis, size):
    core, side = me & 1, (me >> 1) & 1
    if size & (size - 1) or size < 4:
        parts = [jnp.where(core == 0, kept, given), jnp.where(core == 0, given, kept)]
        block = jnp.concatenate(parts, axis=0)
        block = lax.psum(jnp.where(me == owner, block, jnp.zeros_like(block)), axis)
        quarter = block.shape[0] // 4
        places = [(core, side), (core, 1 - side), (1 - core, side), (1 - core, 1 - side)]
        return [
            lax.dynamic_slice_in_dim(block, (2 * first + second) * quarter, quarter, 0)
            for first, second in places
        ]

    def exchange(value, bit):
        return lax.ppermute(value, axis, [(i, i ^ bit) for i in range(size)])

    apart = me ^ owner
    kept = jnp.where(apart == 0, kept, exchange(given, 1))
    middle = kept.shape[0] // 2
    first, second = kept[:middle], kept[middle:]
    kept, given = jnp.where(side == 0, first, second), jnp.where(side == 0, second, first)
    kept = jnp.where(apart < 2, kept, exchange(given, 2))
    bit = 4
    while bit < size:
        kept = jnp.where(apart < bit, kept, exchange(kept, bit))
        bit *= 2
    return [kept] + [exchange(kept, bits) for bits in (2, 1, 3)]


def on_device(
    row_size,
    col_size,
    right_sides,
    pencil_s,
    pencil_t,
    value_alpha,
    value_beta,
    selected,
    block_slot,
    right_basis,
    vectors,
):
    block = pencil_s.shape[1] // 2
    slot_count = right_sides.shape[0] // block
    block_count = block_slot.shape[0]
    rows, _, width = right_basis.shape
    me_row = lax.axis_index("row")
    me_col = lax.axis_index("col")
    slot_upper = block_slot[block_count - 2]
    slot_lower = block_slot[block_count - 1]

    paired = width % 128 == 0
    own = right_basis.reshape((2 * rows, width) if paired else (rows, 2 * width))
    received = [
        lax.ppermute(own, "col", [(i, (i + step) % col_size) for i in range(col_size)])
        for step in range(1, col_size)
    ]
    me = me_row[None]
    parts = jnp.stack([lax.rem(me_col + (col_size - step), col_size) for step in range(col_size)])
    owner_lower, owner_upper = lax.div(slot_lower, slot_count), lax.div(slot_upper, slot_count)
    kept, given, alpha, beta = solve_lower(
        block_slot, me, pencil_s, pencil_t, right_sides, value_alpha, value_beta, selected
    )
    lower = spread(kept, given, me_row, owner_lower, "row", row_size)
    kept, given, lower = solve_upper(
        block_slot, me, pencil_s, pencil_t, right_sides, alpha, beta, lower
    )
    upper = spread(kept, given, me_row, owner_upper, "row", row_size)
    updated_sides, terms = finish_sides(
        block_slot, me, parts, right_sides, pencil_s, pencil_t, alpha, beta, lower, upper
    )
    updated_vectors = add_product(vectors, terms, [own, *received], paired)
    return (updated_sides, updated_vectors)


def solution(mesh):
    body = functools.partial(on_device, mesh.shape["row"], mesh.shape["col"])
    return jax.shard_map(
        body,
        mesh=mesh,
        in_specs=(
            P("row", "col"),
            P("row", None),
            P("row", None),
            P(),
            P(),
            P("col"),
            P(),
            P("row", None, "col"),
            P("row", "col"),
        ),
        out_specs=(P("row", "col"), P("row", "col")),
        check_vma=False,
    )
```

profile of v0, /device:TPU:0, one launch (start us, length us, event | category | flops | bytes accessed | tf_op | source)
XLA Modules:
  0.0 108.8 jit_solution(13094026263447617879)
XLA Ops:
  0.6 3.0 %collective-permute-start.14 = (f32[8192,128]{1,0:T(8,128)}, f32[8192,128]{1,0:T(8,128)}, u32[]{:S(2)}, u32[]{:S(2)}) collective-permute-start(f32[8192,128]{1,0:T(8,128)} %bitcast.9), channel_id=1, source_target_pairs={{0,1},{1,0},{2,3},{3,2},{4,5},{5,4},{6,7},{7,6},{8,9},{9,8},{10,11... | collective-permute-start | bytes 12582920 | tf_op jit(solution)/shard_map/ppermute | solution.py:349
  3.7 7.7 %solve_lower.1 = (f32[128,512]{1,0:T(8,128)}, f32[128,512]{1,0:T(8,128)}, f32[1,512]{1,0:T(1,128)}, f32[1,512]{1,0:T(1,128)}) custom-call(s32[32]{0:T(128)} %slots.5, s32[1]{0:T(128)} %bitcast.me, f32[512,512]{1,0:T(8,128)} %s_ref.5, f32[512,512]{1,0:T(8,128)} %t_ref.5, f32[512,512]{1,0:T(8,128)} %r_ref.5, f32[32,128]{1,0:T(8,128)} %bitcast.11, ...), custom_call_target="tpu_custom_call" | custom-call | flops 1000 | bytes 1000 | tf_op jit(solution)/shard_map/solve_lower/pallas_call | solution.py:146
  11.4 0.0 collective-permute-start
  11.4 1.4 %fusion = (s32[1]{0:T(128)}, s32[1]{0:T(128)}) fusion(s32[32]{0:T(128)} %slots.5), kind=kLoop, calls=%fused_computation.11 | loop fusion | bytes 16 | tf_op jit(solution)/shard_map/slice | solution.py:343
  14.7 0.0 collective-permute-done
  14.8 1.6 %collective-permute-start.1 = (f32[64,512]{1,0:T(8,128)S(1)}, f32[64,512]{1,0:T(8,128)S(1)}, u32[]{:S(2)}, u32[]{:S(2)}) collective-permute-start(f32[64,512]{1,0:T(8,128)S(1)} %slice_select_fusion.1), channel_id=1, source_target_pairs={{0,4},{2,6},{4,0},{6,2},{8,12},{10,14},{12,8},{14,10},{16,20},{18,... | collective-permute-start | bytes 393224 | tf_op jit(solution)/shard_map/ppermute | solution.py:309
  16.3 4.4 %collective-permute-done.1 = f32[64,512]{1,0:T(8,128)S(1)} collective-permute-done((f32[64,512]{1,0:T(8,128)S(1)}, f32[64,512]{1,0:T(8,128)S(1)}, u32[]{:S(2)}, u32[]{:S(2)}) %collective-permute-start.1) | collective-permute-done | bytes 131104 | tf_op jit(solution)/shard_map/ppermute | solution.py:309
  20.8 1.6 %collective-permute-start.2 = (f32[64,512]{1,0:T(8,128)S(1)}, f32[64,512]{1,0:T(8,128)S(1)}, u32[]{:S(2)}, u32[]{:S(2)}) collective-permute-start(f32[64,512]{1,0:T(8,128)S(1)} %select_select_fusion.1), channel_id=1, source_target_pairs={{0,8},{2,10},{4,12},{6,14},{8,0},{10,2},{12,4},{14,6},{16,24},{18,... | collective-permute-start | bytes 393224 | tf_op jit(solution)/shard_map/ppermute | solution.py:309
  22.4 3.7 %collective-permute-done.2 = f32[64,512]{1,0:T(8,128)S(1)} collective-permute-done((f32[64,512]{1,0:T(8,128)S(1)}, f32[64,512]{1,0:T(8,128)S(1)}, u32[]{:S(2)}, u32[]{:S(2)}) %collective-permute-start.2) | collective-permute-done | bytes 131104 | tf_op jit(solution)/shard_map/ppermute | solution.py:309
  26.1 2.6 %collective-permute-start.3 = (f32[64,512]{1,0:T(8,128)S(1)}, f32[64,512]{1,0:T(8,128)S(1)}, u32[]{:S(2)}, u32[]{:S(2)}) collective-permute-start(f32[64,512]{1,0:T(8,128)S(1)} %broadcast_select_fusion.4), channel_id=1, source_target_pairs={{0,16},{2,18},{4,20},{6,22},{8,24},{10,26},{12,28},{14,30},{16,0},... | collective-permute-start | bytes 393224 | tf_op jit(solution)/shard_map/ppermute | solution.py:309
  28.7 5.6 %collective-permute-done.3 = f32[64,512]{1,0:T(8,128)S(1)} collective-permute-done((f32[64,512]{1,0:T(8,128)S(1)}, f32[64,512]{1,0:T(8,128)S(1)}, u32[]{:S(2)}, u32[]{:S(2)}) %collective-permute-start.3) | collective-permute-done | bytes 131104 | tf_op jit(solution)/shard_map/ppermute | solution.py:309
  34.4 0.0 copy-start.3
  34.4 0.1 collective-permute-start.6
  34.5 1.6 %collective-permute-start.5 = (f32[64,512]{1,0:T(8,128)S(1)}, f32[64,512]{1,0:T(8,128)S(1)}, u32[]{:S(2)}, u32[]{:S(2)}) collective-permute-start(f32[64,512]{1,0:T(8,128)S(1)} %broadcast_select_fusion.5.refs_0_), channel_id=1, source_target_pairs={{0,2},{2,0},{4,6},{6,4},{8,10},{10,8},{12,14},{14,12},{16,18},{18,... | collective-permute-start | bytes 393224 | tf_op jit(solution)/shard_map/ppermute | solution.py:309
  36.0 0.5 collective-permute-start.4
  36.6 3.6 %collective-permute-done.6.refs_3_ = f32[64,512]{1,0:T(8,128)S(1)} collective-permute-done((f32[64,512]{1,0:T(8,128)S(1)}, f32[64,512]{1,0:T(8,128)S(1)}, u32[]{:S(2)}, u32[]{:S(2)}) %collective-permute-start.6) | collective-permute-done | bytes 131104 | tf_op jit(solution)/shard_map/ppermute | solution.py:309
  40.2 0.0 copy-start.7
  40.2 0.0 collective-permute-done.5.refs_2_
  40.2 0.0 copy-start.8
  40.2 2.9 %collective-permute-done.4.refs_1_ = f32[64,512]{1,0:T(8,128)S(1)} collective-permute-done((f32[64,512]{1,0:T(8,128)S(1)}, f32[64,512]{1,0:T(8,128)S(1)}, u32[]{:S(2)}, u32[]{:S(2)}) %collective-permute-start.4) | collective-permute-done | bytes 131104 | tf_op jit(solution)/shard_map/ppermute | solution.py:309
  43.0 0.0 copy-start.9
  43.0 0.0 copy-done.3
  43.0 0.0 copy-done.7
  43.0 0.0 copy-done.8
  43.0 0.6 copy-done.9
  43.7 8.6 %solve_upper.1 = (f32[128,512]{1,0:T(8,128)}, f32[128,512]{1,0:T(8,128)}, f32[256,512]{1,0:T(8,128)}) custom-call(s32[32]{0:T(128)} %slots.5, s32[1]{0:T(128)} %bitcast.me, f32[512,512]{1,0:T(8,128)} %s_ref.5, f32[512,512]{1,0:T(8,128)} %t_ref.5, f32[512,512]{1,0:T(8,128)} %r_ref.5, f32[1,512]{1,0:T(1,128)} %get-tuple-element.11.alpha_ref, ...), custom_call_target="tpu_custom_call" | custom-call | flops 1000 | bytes 1000 | tf_op jit(solution)/shard_map/solve_upper/pallas_call | solution.py:182
  52.3 0.2 collective-permute-start.7
  54.5 0.0 collective-permute-done.7
  54.6 1.7 %collective-permute-start.8 = (f32[64,512]{1,0:T(8,128)S(1)}, f32[64,512]{1,0:T(8,128)S(1)}, u32[]{:S(2)}, u32[]{:S(2)}) collective-permute-start(f32[64,512]{1,0:T(8,128)S(1)} %slice_select_fusion), channel_id=1, source_target_pairs={{0,4},{2,6},{4,0},{6,2},{8,12},{10,14},{12,8},{14,10},{16,20},{18,... | collective-permute-start | bytes 393224 | tf_op jit(solution)/shard_map/ppermute | solution.py:309
  56.3 4.1 %collective-permute-done.8 = f32[64,512]{1,0:T(8,128)S(1)} collective-permute-done((f32[64,512]{1,0:T(8,128)S(1)}, f32[64,512]{1,0:T(8,128)S(1)}, u32[]{:S(2)}, u32[]{:S(2)}) %collective-permute-start.8) | collective-permute-done | bytes 131104 | tf_op jit(solution)/shard_map/ppermute | solution.py:309
  60.5 0.1 collective-permute-start.9
  60.6 5.0 %collective-permute-done.9 = f32[64,512]{1,0:T(8,128)S(1)} collective-permute-done((f32[64,512]{1,0:T(8,128)S(1)}, f32[64,512]{1,0:T(8,128)S(1)}, u32[]{:S(2)}, u32[]{:S(2)}) %collective-permute-start.9) | collective-permute-done | bytes 131104 | tf_op jit(solution)/shard_map/ppermute | solution.py:309
  65.6 1.5 %collective-permute-start.10 = (f32[64,512]{1,0:T(8,128)S(1)}, f32[64,512]{1,0:T(8,128)S(1)}, u32[]{:S(2)}, u32[]{:S(2)}) collective-permute-start(f32[64,512]{1,0:T(8,128)S(1)} %broadcast_select_fusion.2), channel_id=1, source_target_pairs={{0,16},{2,18},{4,20},{6,22},{8,24},{10,26},{12,28},{14,30},{16,0},... | collective-permute-start | bytes 393224 | tf_op jit(solution)/shard_map/ppermute | solution.py:309
  67.1 6.5 %collective-permute-done.10 = f32[64,512]{1,0:T(8,128)S(1)} collective-permute-done((f32[64,512]{1,0:T(8,128)S(1)}, f32[64,512]{1,0:T(8,128)S(1)}, u32[]{:S(2)}, u32[]{:S(2)}) %collective-permute-start.10) | collective-permute-done | bytes 131104 | tf_op jit(solution)/shard_map/ppermute | solution.py:309
  73.7 0.0 copy-start.2
  73.7 0.1 collective-permute-start.13
  73.8 0.3 collective-permute-start.12
  74.1 1.8 %collective-permute-start.11 = (f32[64,512]{1,0:T(8,128)S(1)}, f32[64,512]{1,0:T(8,128)S(1)}, u32[]{:S(2)}, u32[]{:S(2)}) collective-permute-start(f32[64,512]{1,0:T(8,128)S(1)} %broadcast_select_fusion.3.refs_0_), channel_id=1, source_target_pairs={{0,4},{2,6},{4,0},{6,2},{8,12},{10,14},{12,8},{14,10},{16,20},{18,... | collective-permute-start | bytes 393224 | tf_op jit(solution)/shard_map/ppermute | solution.py:309
  75.9 0.0 copy-start
  75.9 0.7 pad_add_fusion.parts
  76.5 3.0 %collective-permute-done.13.refs_3_ = f32[64,512]{1,0:T(8,128)S(1)} collective-permute-done((f32[64,512]{1,0:T(8,128)S(1)}, f32[64,512]{1,0:T(8,128)S(1)}, u32[]{:S(2)}, u32[]{:S(2)}) %collective-permute-start.13) | collective-permute-done | bytes 131104 | tf_op jit(solution)/shard_map/ppermute | solution.py:309
  79.5 0.0 copy-start.4
  79.5 0.0 collective-permute-done.12.refs_2_
  79.5 0.0 copy-start.5
  79.5 2.4 %collective-permute-done.11.refs_1_ = f32[64,512]{1,0:T(8,128)S(1)} collective-permute-done((f32[64,512]{1,0:T(8,128)S(1)}, f32[64,512]{1,0:T(8,128)S(1)}, u32[]{:S(2)}, u32[]{:S(2)}) %collective-permute-start.11) | collective-permute-done | bytes 131104 | tf_op jit(solution)/shard_map/ppermute | solution.py:309
  81.9 0.0 copy-start.6
  81.9 0.0 copy-done.2
  81.9 0.0 copy-done.4
  81.9 0.0 copy-done.5
  81.9 0.6 copy-done.6
  82.6 5.6 %finish_sides.1 = (f32[512,512]{1,0:T(8,128)}, bf16[1536,512]{1,0:T(8,128)(2,1)}) custom-call(s32[32]{0:T(128)} %slots.5, s32[1]{0:T(128)} %bitcast.me, s32[2]{0:T(128)} %pad_add_fusion.parts, f32[512,512]{1,0:T(8,128)} %r_ref.5, f32[512,512]{1,0:T(8,128)} %s_ref.5, f32[512,512]{1,0:T(8,128)} %t_ref.5, f32[1,512]{1,0:T(1,128)} %get-tuple-element.11.alpha_ref, ...), custom_call_target="tpu_custom_call" | custom-call | flops 1000 | bytes 1000 | tf_op jit(solution)/shard_map/finish_sides/pallas_call | solution.py:245
  88.2 6.4 %collective-permute-done.14.refs_1_ = f32[8192,128]{1,0:T(8,128)} collective-permute-done((f32[8192,128]{1,0:T(8,128)}, f32[8192,128]{1,0:T(8,128)}, u32[]{:S(2)}, u32[]{:S(2)}) %collective-permute-start.14) | collective-permute-done | bytes 4194336 | tf_op jit(solution)/shard_map/ppermute | solution.py:349
  94.6 0.0 copy-done
  94.6 0.0 copy-start.1
  94.6 1.4 %copy-done.1 = bf16[1536,512]{1,0:T(8,128)(2,1)S(1)} copy-done((bf16[1536,512]{1,0:T(8,128)(2,1)S(1)}, bf16[1536,512]{1,0:T(8,128)(2,1)}, u32[]{:S(2)}) %copy-start.1) | copy-done | bytes 1572888
  96.0 12.8 %add_product.1 = f32[4096,512]{1,0:T(8,128)} custom-call(f32[4096,512]{1,0:T(8,128)} %base_ref.1, bf16[1536,512]{1,0:T(8,128)(2,1)S(1)} %copy-done.1, f32[8192,128]{1,0:T(8,128)S(1)} %bitcast.10, f32[8192,128]{1,0:T(8,128)} %collective-permute-done.14.refs_1_), custom_call_target="tpu_custom_call" | custom-call | flops 1000 | bytes 1000 | tf_op jit(solution)/shard_map/add_product/pallas_call | solution.py:282
  (10 shorter events, 0.3 us)
Async XLA Ops:
  0.6 93.9 %collective-permute-start.14 = (f32[8192,128]{1,0:T(8,128)}, f32[8192,128]{1,0:T(8,128)}, u32[]{:S(2)}, u32[]{:S(2)}) collective-permute-start(f32[8192,128]{1,0:T(8,128)} %bitcast.9), channel_id=1, source_target_pairs={{0,1},{1,0},{2,3},{3,2},{4,5},{5,4},{6,7},{7,6},{8,9},{9,8},{10,11... | collective-permute-start | bytes 12582920 | tf_op jit(solution)/shard_map/ppermute | solution.py:349
  11.4 3.3 %collective-permute-start = (f32[128,512]{1,0:T(8,128)}, f32[128,512]{1,0:T(8,128)S(1)}, u32[]{:S(2)}, u32[]{:S(2)}) collective-permute-start(f32[128,512]{1,0:T(8,128)} %get-tuple-element.14), channel_id=1, source_target_pairs={{0,2},{2,0},{4,6},{6,4},{8,10},{10,8},{12,14},{14,12},{16,18},{18,... | collective-permute-start | bytes 786440 | tf_op jit(solution)/shard_map/ppermute | solution.py:309
  14.8 6.0 %collective-permute-start.1 = (f32[64,512]{1,0:T(8,128)S(1)}, f32[64,512]{1,0:T(8,128)S(1)}, u32[]{:S(2)}, u32[]{:S(2)}) collective-permute-start(f32[64,512]{1,0:T(8,128)S(1)} %slice_select_fusion.1), channel_id=1, source_target_pairs={{0,4},{2,6},{4,0},{6,2},{8,12},{10,14},{12,8},{14,10},{16,20},{18,... | collective-permute-start | bytes 393224 | tf_op jit(solution)/shard_map/ppermute | solution.py:309
  20.8 5.3 %collective-permute-start.2 = (f32[64,512]{1,0:T(8,128)S(1)}, f32[64,512]{1,0:T(8,128)S(1)}, u32[]{:S(2)}, u32[]{:S(2)}) collective-permute-start(f32[64,512]{1,0:T(8,128)S(1)} %select_select_fusion.1), channel_id=1, source_target_pairs={{0,8},{2,10},{4,12},{6,14},{8,0},{10,2},{12,4},{14,6},{16,24},{18,... | collective-permute-start | bytes 393224 | tf_op jit(solution)/shard_map/ppermute | solution.py:309
  26.1 8.2 %collective-permute-start.3 = (f32[64,512]{1,0:T(8,128)S(1)}, f32[64,512]{1,0:T(8,128)S(1)}, u32[]{:S(2)}, u32[]{:S(2)}) collective-permute-start(f32[64,512]{1,0:T(8,128)S(1)} %broadcast_select_fusion.4), channel_id=1, source_target_pairs={{0,16},{2,18},{4,20},{6,22},{8,24},{10,26},{12,28},{14,30},{16,0},... | collective-permute-start | bytes 393224 | tf_op jit(solution)/shard_map/ppermute | solution.py:309
  34.4 8.7 %copy-start.3 = (f32[64,512]{1,0:T(8,128)}, f32[64,512]{1,0:T(8,128)S(1)}, u32[]{:S(2)}) copy-start(f32[64,512]{1,0:T(8,128)S(1)} %broadcast_select_fusion.5.refs_0_) | copy-start | bytes 393220
  34.4 5.8 %collective-permute-start.6 = (f32[64,512]{1,0:T(8,128)S(1)}, f32[64,512]{1,0:T(8,128)S(1)}, u32[]{:S(2)}, u32[]{:S(2)}) collective-permute-start(f32[64,512]{1,0:T(8,128)S(1)} %broadcast_select_fusion.5.refs_0_), channel_id=1, source_target_pairs={{0,6},{2,4},{4,2},{6,0},{8,14},{10,12},{12,10},{14,8},{16,22},{18,... | collective-permute-start | bytes 393224 | tf_op jit(solution)/shard_map/ppermute | solution.py:309
  34.5 5.7 %collective-permute-start.5 = (f32[64,512]{1,0:T(8,128)S(1)}, f32[64,512]{1,0:T(8,128)S(1)}, u32[]{:S(2)}, u32[]{:S(2)}) collective-permute-start(f32[64,512]{1,0:T(8,128)S(1)} %broadcast_select_fusion.5.refs_0_), channel_id=1, source_target_pairs={{0,2},{2,0},{4,6},{6,4},{8,10},{10,8},{12,14},{14,12},{16,18},{18,... | collective-permute-start | bytes 393224 | tf_op jit(solution)/shard_map/ppermute | solution.py:309
  36.0 7.0 %collective-permute-start.4 = (f32[64,512]{1,0:T(8,128)S(1)}, f32[64,512]{1,0:T(8,128)S(1)}, u32[]{:S(2)}, u32[]{:S(2)}) collective-permute-start(f32[64,512]{1,0:T(8,128)S(1)} %broadcast_select_fusion.5.refs_0_), channel_id=1, source_target_pairs={{0,4},{2,6},{4,0},{6,2},{8,12},{10,14},{12,8},{14,10},{16,20},{18,... | collective-permute-start | bytes 393224 | tf_op jit(solution)/shard_map/ppermute | solution.py:309
  40.2 2.9 %copy-start.7 = (f32[64,512]{1,0:T(8,128)}, f32[64,512]{1,0:T(8,128)S(1)}, u32[]{:S(2)}) copy-start(f32[64,512]{1,0:T(8,128)S(1)} %collective-permute-done.6.refs_3_) | copy-start | bytes 393220
  40.2 2.9 %copy-start.8 = (f32[64,512]{1,0:T(8,128)}, f32[64,512]{1,0:T(8,128)S(1)}, u32[]{:S(2)}) copy-start(f32[64,512]{1,0:T(8,128)S(1)} %collective-permute-done.5.refs_2_) | copy-start | bytes 393220
  43.0 0.6 copy-start.9
  52.3 2.2 %collective-permute-start.7 = (f32[128,512]{1,0:T(8,128)}, f32[128,512]{1,0:T(8,128)S(1)}, u32[]{:S(2)}, u32[]{:S(2)}) collective-permute-start(f32[128,512]{1,0:T(8,128)} %get-tuple-element.17), channel_id=1, source_target_pairs={{0,2},{2,0},{4,6},{6,4},{8,10},{10,8},{12,14},{14,12},{16,18},{18,... | collective-permute-start | bytes 786440 | tf_op jit(solution)/shard_map/ppermute | solution.py:309
  54.6 5.8 %collective-permute-start.8 = (f32[64,512]{1,0:T(8,128)S(1)}, f32[64,512]{1,0:T(8,128)S(1)}, u32[]{:S(2)}, u32[]{:S(2)}) collective-permute-start(f32[64,512]{1,0:T(8,128)S(1)} %slice_select_fusion), channel_id=1, source_target_pairs={{0,4},{2,6},{4,0},{6,2},{8,12},{10,14},{12,8},{14,10},{16,20},{18,... | collective-permute-start | bytes 393224 | tf_op jit(solution)/shard_map/ppermute | solution.py:309
  60.5 5.1 %collective-permute-start.9 = (f32[64,512]{1,0:T(8,128)S(1)}, f32[64,512]{1,0:T(8,128)S(1)}, u32[]{:S(2)}, u32[]{:S(2)}) collective-permute-start(f32[64,512]{1,0:T(8,128)S(1)} %select_select_fusion), channel_id=1, source_target_pairs={{0,8},{2,10},{4,12},{6,14},{8,0},{10,2},{12,4},{14,6},{16,24},{18,... | collective-permute-start | bytes 393224 | tf_op jit(solution)/shard_map/ppermute | solution.py:309
  65.6 8.0 %collective-permute-start.10 = (f32[64,512]{1,0:T(8,128)S(1)}, f32[64,512]{1,0:T(8,128)S(1)}, u32[]{:S(2)}, u32[]{:S(2)}) collective-permute-start(f32[64,512]{1,0:T(8,128)S(1)} %broadcast_select_fusion.2), channel_id=1, source_target_pairs={{0,16},{2,18},{4,20},{6,22},{8,24},{10,26},{12,28},{14,30},{16,0},... | collective-permute-start | bytes 393224 | tf_op jit(solution)/shard_map/ppermute | solution.py:309
  73.7 8.3 %copy-start.2 = (f32[64,512]{1,0:T(8,128)}, f32[64,512]{1,0:T(8,128)S(1)}, u32[]{:S(2)}) copy-start(f32[64,512]{1,0:T(8,128)S(1)} %broadcast_select_fusion.3.refs_0_) | copy-start | bytes 393220
  73.7 5.9 %collective-permute-start.13 = (f32[64,512]{1,0:T(8,128)S(1)}, f32[64,512]{1,0:T(8,128)S(1)}, u32[]{:S(2)}, u32[]{:S(2)}) collective-permute-start(f32[64,512]{1,0:T(8,128)S(1)} %broadcast_select_fusion.3.refs_0_), channel_id=1, source_target_pairs={{0,6},{2,4},{4,2},{6,0},{8,14},{10,12},{12,10},{14,8},{16,22},{18,... | collective-permute-start | bytes 393224 | tf_op jit(solution)/shard_map/ppermute | solution.py:309
  73.8 5.8 %collective-permute-start.12 = (f32[64,512]{1,0:T(8,128)S(1)}, f32[64,512]{1,0:T(8,128)S(1)}, u32[]{:S(2)}, u32[]{:S(2)}) collective-permute-start(f32[64,512]{1,0:T(8,128)S(1)} %broadcast_select_fusion.3.refs_0_), channel_id=1, source_target_pairs={{0,2},{2,0},{4,6},{6,4},{8,10},{10,8},{12,14},{14,12},{16,18},{18,... | collective-permute-start | bytes 393224 | tf_op jit(solution)/shard_map/ppermute | solution.py:309
  74.1 7.9 %collective-permute-start.11 = (f32[64,512]{1,0:T(8,128)S(1)}, f32[64,512]{1,0:T(8,128)S(1)}, u32[]{:S(2)}, u32[]{:S(2)}) collective-permute-start(f32[64,512]{1,0:T(8,128)S(1)} %broadcast_select_fusion.3.refs_0_), channel_id=1, source_target_pairs={{0,4},{2,6},{4,0},{6,2},{8,12},{10,14},{12,8},{14,10},{16,20},{18,... | collective-permute-start | bytes 393224 | tf_op jit(solution)/shard_map/ppermute | solution.py:309
  75.9 18.7 %copy-start = (f32[4096,2,128]{2,1,0:T(2,128)S(1)}, f32[4096,2,128]{2,1,0:T(2,128)}, u32[]{:S(2)}) copy-start(f32[4096,2,128]{2,1,0:T(2,128)} %param.16) | copy-start | bytes 12582916
  79.5 2.4 %copy-start.4 = (f32[64,512]{1,0:T(8,128)}, f32[64,512]{1,0:T(8,128)S(1)}, u32[]{:S(2)}) copy-start(f32[64,512]{1,0:T(8,128)S(1)} %collective-permute-done.13.refs_3_) | copy-start | bytes 393220
  79.5 2.4 %copy-start.5 = (f32[64,512]{1,0:T(8,128)}, f32[64,512]{1,0:T(8,128)S(1)}, u32[]{:S(2)}) copy-start(f32[64,512]{1,0:T(8,128)S(1)} %collective-permute-done.12.refs_2_) | copy-start | bytes 393220
  81.9 0.6 copy-start.6
  94.6 1.4 %copy-start.1 = (bf16[1536,512]{1,0:T(8,128)(2,1)S(1)}, bf16[1536,512]{1,0:T(8,128)(2,1)}, u32[]{:S(2)}) copy-start(bf16[1536,512]{1,0:T(8,128)(2,1)} %get-tuple-element.19.terms_ref) | copy-start | bytes 4718596
where the time goes:
time: 109 us
  waiting for transfers between devices  47.5 us (44%)
  Pallas kernels  34.8 us (32%)
  starting transfers between devices  16.7 us (15%)
  between operations  4.76 us (4%)
  local copies, waits for them, and re-layouts  4.1 us (4%)
    ppermute x14, waiting for transfers between devices, exchange(): return lax.ppermute(value, axis, [(i, i ^ bit) for i in range(size)])  41.2 us
    ppermute x14, starting transfers between devices, exchange(): return lax.ppermute(value, axis, [(i, i ^ bit) for i in range(size)])  13.7 us
    pallas_call x1, Pallas kernels, add_product(): pl.pallas_call(functools.partial(add_kernel, paired), out_shape=jax.Shape...  12.8 us
    pallas_call x1, Pallas kernels, solve_upper(): pl.pallas_call(upper_kernel, out_shape=(*[jax.ShapeDtypeStruct((block //...  8.62 us
    pallas_call x1, Pallas kernels, solve_lower(): pl.pallas_call(lower_kernel, out_shape=(*[jax.ShapeDtypeStruct((block //...  7.7 us
    ppermute x1, waiting for transfers between devices, on_device(): lax.ppermute(own, 'col', [(i, (i + step) % col_size) for i in range(col_s...  6.38 us
    pallas_call x1, Pallas kernels, finish_sides(): pl.pallas_call(finish_kernel, out_shape=(jax.ShapeDtypeStruct(sides.shape...  5.61 us
    ppermute x1, starting transfers between devices, on_device(): lax.ppermute(own, 'col', [(i, (i + step) % col_size) for i in range(col_s...  3.03 us
  transfers between devices with their start and end apart: 15, of which 11 were waited for; matrix products, arithmetic and copies ran while one was open for 2% of the time, Pallas kernels for 20%

commit v1 on v0

--- a/solution.py
+++ b/solution.py
@@ -11,7 +11,7 @@
 SUB = 32
 GROUP = 8
 VMEM_BYTES = 57 * 1024 * 1024
-ADD_VMEM_BYTES = 48 * 1024 * 1024
+ADD_VMEM_BYTES = 36 * 1024 * 1024
 FULL_VMEM_BYTES = 59 * 1024 * 1024
 TILE = 512
 LIGHT = pl.CostEstimate(flops=1000, bytes_accessed=1000, transcendentals=0)
@@ -214,17 +214,18 @@
 
 
 def finish_kernel(slots, me, parts, r_ref, s_ref, t_ref, alpha_ref, beta_ref, lower_ref, *refs):
-    piece_refs, (out_ref, terms_ref, upper_ref) = refs[:4], refs[4:]
+    piece_refs, (out_ref, own_terms, other_terms, upper_ref) = refs[:4], refs[4:]
     put_together(me[0] & 1, (me[0] >> 1) & 1, piece_refs, upper_ref)
     block = upper_ref.shape[0]
     width = block // parts.shape[0]
     for part in range(parts.shape[0]):
         rows = pl.ds(pl.multiple_of(parts[part] * width, width), width)
+        terms_ref = other_terms if part else own_terms
         for half, source in enumerate((upper_ref, lower_ref)):
-            target = (2 * part + half) * width
+            target = (2 * max(part - 1, 0) + half) * width
             high, low = split_two(source[rows, :])
             for term, value in enumerate((high, high, low)):
-                first = 2 * block * term + target
+                first = terms_ref.shape[0] // 3 * term + target
                 terms_ref[first : first + width, :] = value
     count = out_ref.shape[0] // block
     base = me[0] * count
@@ -241,15 +242,17 @@
 
 def finish_sides(slots, me, parts, sides, pencil_s, pencil_t, alpha, beta, lower, pieces):
     block, eigs = lower.shape
+    width = block // parts.shape[0]
     smem, vmem = pl.BlockSpec(memory_space=pltpu.SMEM), pl.BlockSpec(memory_space=pltpu.VMEM)
     return pl.pallas_call(
         finish_kernel,
         out_shape=(
             jax.ShapeDtypeStruct(sides.shape, jnp.float32),
-            jax.ShapeDtypeStruct((6 * block, eigs), jnp.bfloat16),
+            jax.ShapeDtypeStruct((6 * width, eigs), jnp.bfloat16),
+            jax.ShapeDtypeStruct((6 * (block - width), eigs), jnp.bfloat16),
         ),
         in_specs=[smem] * 3 + [vmem] * (6 + len(pieces)),
-        out_specs=(vmem, vmem),
+        out_specs=(vmem, vmem, vmem),
         scratch_shapes=[pltpu.VMEM((block, eigs), jnp.float32)],
         compiler_params=pltpu.CompilerParams(vmem_limit_bytes=VMEM_BYTES),
         cost_estimate=LIGHT,
@@ -257,39 +260,37 @@
     )(slots, me, parts, sides, pencil_s, pencil_t, alpha, beta, lower, *pieces)
 
 
-def add_kernel(paired, base_ref, terms_ref, *refs):
-    part_refs, out_ref = refs[: len(refs) - 1], refs[-1]
-    tile = out_ref.shape[0]
-    pieces = []
-    for ref in part_refs:
-        if paired:
-            pieces.append(ref[pl.ds(0, tile, 2), :])
-            pieces.append(ref[pl.ds(1, tile, 2), :])
-        else:
-            pieces.append(ref[...])
-    basis = jnp.concatenate(pieces, axis=1)
-    out_ref[...] = base_ref[...] + near_dot(basis, terms_ref[...])
-
-
-def add_product(vectors, terms, parts, paired):
-    rows, eigs = vectors.shape
+def add_kernel(paired, held, base_ref, terms_ref, *refs):
+    part_refs, out_ref = refs[:-1], refs[-1]
+    tile = part_refs[0].shape[0] // (2 if paired else 1)
+    if paired:
+        pieces = [ref[pl.ds(half, tile, 2), :] for ref in part_refs for half in range(2)]
+    else:
+        pieces = [ref[...] for ref in part_refs]
+    product = near_dot(jnp.concatenate(pieces, axis=1), terms_ref[...])
+    whole = pl.ds(pl.multiple_of(pl.program_id(0) * tile, tile), tile)
+    if held == "out":
+        out_ref[whole, :] = base_ref[...] + product
+    else:
+        out_ref[...] = base_ref[whole, :] + product
+
+
+def add_product(base, terms, parts, paired, held):
+    rows, eigs = base.shape
     tile = math.gcd(TILE, rows)
     per, width = parts[0].shape[0] // rows, parts[0].shape[1]
-
-    def stream(height, lanes):
-        return pl.BlockSpec((height, lanes), lambda i: (i, 0))
-
+    tiles, vmem = pl.BlockSpec((tile, eigs), lambda i: (i, 0)), pl.BlockSpec(memory_space=pltpu.VMEM)
     return pl.pallas_call(
-        functools.partial(add_kernel, paired),
+        functools.partial(add_kernel, paired, held),
         out_shape=jax.ShapeDtypeStruct((rows, eigs), jnp.float32),
         grid=(rows // tile,),
-        in_specs=[stream(tile, eigs), pl.BlockSpec(memory_space=pltpu.VMEM)]
-        + [stream(per * tile, width) for _ in parts],
-        out_specs=pl.BlockSpec((tile, eigs), lambda i: (i, 0)),
+        in_specs=[vmem if held == "base" else tiles, vmem]
+        + [pl.BlockSpec((per * tile, width), lambda i: (i, 0)) for _ in parts],
+        out_specs=vmem if held == "out" else tiles,
         compiler_params=pltpu.CompilerParams(vmem_limit_bytes=ADD_VMEM_BYTES),
         cost_estimate=LIGHT,
-        name="add_product",
-    )(vectors, terms, *parts)
+        name="add_own" if held == "out" else "add_received",
+    )(base, terms, *parts)
 
 
 def spread(kept, given, me, owner, axis, size):
@@ -360,10 +361,11 @@
         block_slot, me, pencil_s, pencil_t, right_sides, alpha, beta, lower
     )
     upper = spread(kept, given, me_row, owner_upper, "row", row_size)
-    updated_sides, terms = finish_sides(
+    updated_sides, own_terms, other_terms = finish_sides(
         block_slot, me, parts, right_sides, pencil_s, pencil_t, alpha, beta, lower, upper
     )
-    updated_vectors = add_product(vectors, terms, [own, *received], paired)
+    updated_vectors = add_product(vectors, own_terms, [own], paired, "out")
+    updated_vectors = add_product(updated_vectors, other_terms, received, paired, "base")
     return (updated_sides, updated_vectors)
 
 

time: 109 us -> 110 us (level)
  waiting for transfers between devices: 47.5 us -> 41.2 us
  Pallas kernels: 34.8 us -> 39.3 us
  local copies, waits for them, and re-layouts: 4.1 us -> 6 us
    ppermute x1, waiting for transfers between devices: 6.38 us -> 0.01 us  [on_device(): lax.ppermute(own, 'col', [(i, (i + step) % col_size) for i in range(col_s...]
    pallas_call x1 -> x2, Pallas kernels: 12.8 us -> 17.4 us  [add_product(): pl.pallas_call(functools.partial(add_kernel, paired, held), out_shape=jax...]
    unnamed x20 -> x22, local copies, waits for them, and re-layouts: 2.71 us -> 4.62 us
  transfers between devices with their start and end apart: 15 -> 15, of which waited for: 11 -> 10; matrix products, arithmetic and copies ran while one was open for 2% -> 2% of each run, Pallas kernels for 20% -> 28%
where the time goes in v1:
time: 110 us; the launch traced here: 109 us
  waiting for transfers between devices  41.2 us (37%)
  Pallas kernels  39.3 us (36%)
  starting transfers between devices  17.1 us (16%)
  local copies, waits for them, and re-layouts  6 us (5%)
  between operations  4.74 us (4%)
    ppermute x14, waiting for transfers between devices, exchange(): return lax.ppermute(value, axis, [(i, i ^ bit) for i in range(size)])  41.2 us
    pallas_call x2, Pallas kernels, add_product(): pl.pallas_call(functools.partial(add_kernel, paired, held), out_shape=jax...  17.4 us
    ppermute x14, starting transfers between devices, exchange(): return lax.ppermute(value, axis, [(i, i ^ bit) for i in range(size)])  14.1 us
    pallas_call x1, Pallas kernels, solve_upper(): pl.pallas_call(upper_kernel, out_shape=(*[jax.ShapeDtypeStruct((block //...  8.65 us
    pallas_call x1, Pallas kernels, solve_lower(): pl.pallas_call(lower_kernel, out_shape=(*[jax.ShapeDtypeStruct((block //...  7.7 us
    pallas_call x1, Pallas kernels, finish_sides(): pl.pallas_call(finish_kernel, out_shape=(jax.ShapeDtypeStruct(sides.shape...  5.61 us
    unnamed x22, local copies, waits for them, and re-layouts  4.62 us
    ppermute x1, starting transfers between devices, on_device(): lax.ppermute(own, 'col', [(i, (i + step) % col_size) for i in range(col_s...  3.03 us
  transfers between devices with their start and end apart: 15, of which 10 were waited for; matrix products, arithmetic and copies ran while one was open for 2% of the time, Pallas kernels for 28%

profile of v1, /device:TPU:0, one launch (start us, length us, event | category | flops | bytes accessed | tf_op | source)
XLA Modules:
  0.0 109.3 jit_solution(18428819492078268564)
XLA Ops:
  0.6 3.0 %collective-permute-start.14 = (f32[8192,128]{1,0:T(8,128)}, f32[8192,128]{1,0:T(8,128)}, u32[]{:S(2)}, u32[]{:S(2)}) collective-permute-start(f32[8192,128]{1,0:T(8,128)} %bitcast.9), channel_id=1, source_target_pairs={{0,1},{1,0},{2,3},{3,2},{4,5},{5,4},{6,7},{7,6},{8,9},{9,8},{10,11... | collective-permute-start | bytes 12582920 | tf_op jit(solution)/shard_map/ppermute | solution.py:350
  3.7 7.7 %solve_lower.1 = (f32[128,512]{1,0:T(8,128)}, f32[128,512]{1,0:T(8,128)}, f32[1,512]{1,0:T(1,128)}, f32[1,512]{1,0:T(1,128)}) custom-call(s32[32]{0:T(128)} %slots.5, s32[1]{0:T(128)} %bitcast.me, f32[512,512]{1,0:T(8,128)} %s_ref.5, f32[512,512]{1,0:T(8,128)} %t_ref.5, f32[512,512]{1,0:T(8,128)} %r_ref.5, f32[32,128]{1,0:T(8,128)} %bitcast.11, ...), custom_call_target="tpu_custom_call" | custom-call | flops 1000 | bytes 1000 | tf_op jit(solution)/shard_map/solve_lower/pallas_call | solution.py:146
  11.4 0.0 collective-permute-start
  11.4 1.4 %fusion = (s32[1]{0:T(128)}, s32[1]{0:T(128)}) fusion(s32[32]{0:T(128)} %slots.5), kind=kLoop, calls=%fused_computation.11 | loop fusion | bytes 16 | tf_op jit(solution)/shard_map/slice | solution.py:344
  14.8 0.0 collective-permute-done
  14.9 1.6 %collective-permute-start.1 = (f32[64,512]{1,0:T(8,128)S(1)}, f32[64,512]{1,0:T(8,128)S(1)}, u32[]{:S(2)}, u32[]{:S(2)}) collective-permute-start(f32[64,512]{1,0:T(8,128)S(1)} %slice_select_fusion.1), channel_id=1, source_target_pairs={{0,4},{2,6},{4,0},{6,2},{8,12},{10,14},{12,8},{14,10},{16,20},{18,... | collective-permute-start | bytes 393224 | tf_op jit(solution)/shard_map/ppermute | solution.py:310
  16.5 4.4 %collective-permute-done.1 = f32[64,512]{1,0:T(8,128)S(1)} collective-permute-done((f32[64,512]{1,0:T(8,128)S(1)}, f32[64,512]{1,0:T(8,128)S(1)}, u32[]{:S(2)}, u32[]{:S(2)}) %collective-permute-start.1) | collective-permute-done | bytes 131104 | tf_op jit(solution)/shard_map/ppermute | solution.py:310
  20.9 1.7 %collective-permute-start.2 = (f32[64,512]{1,0:T(8,128)S(1)}, f32[64,512]{1,0:T(8,128)S(1)}, u32[]{:S(2)}, u32[]{:S(2)}) collective-permute-start(f32[64,512]{1,0:T(8,128)S(1)} %select_select_fusion.1), channel_id=1, source_target_pairs={{0,8},{2,10},{4,12},{6,14},{8,0},{10,2},{12,4},{14,6},{16,24},{18,... | collective-permute-start | bytes 393224 | tf_op jit(solution)/shard_map/ppermute | solution.py:310
  22.6 4.3 %collective-permute-done.2 = f32[64,512]{1,0:T(8,128)S(1)} collective-permute-done((f32[64,512]{1,0:T(8,128)S(1)}, f32[64,512]{1,0:T(8,128)S(1)}, u32[]{:S(2)}, u32[]{:S(2)}) %collective-permute-start.2) | collective-permute-done | bytes 131104 | tf_op jit(solution)/shard_map/ppermute | solution.py:310
  26.9 2.0 %collective-permute-start.3 = (f32[64,512]{1,0:T(8,128)S(1)}, f32[64,512]{1,0:T(8,128)S(1)}, u32[]{:S(2)}, u32[]{:S(2)}) collective-permute-start(f32[64,512]{1,0:T(8,128)S(1)} %broadcast_select_fusion.4), channel_id=1, source_target_pairs={{0,16},{2,18},{4,20},{6,22},{8,24},{10,26},{12,28},{14,30},{16,0},... | collective-permute-start | bytes 393224 | tf_op jit(solution)/shard_map/ppermute | solution.py:310
  28.9 7.1 %collective-permute-done.3 = f32[64,512]{1,0:T(8,128)S(1)} collective-permute-done((f32[64,512]{1,0:T(8,128)S(1)}, f32[64,512]{1,0:T(8,128)S(1)}, u32[]{:S(2)}, u32[]{:S(2)}) %collective-permute-start.3) | collective-permute-done | bytes 131104 | tf_op jit(solution)/shard_map/ppermute | solution.py:310
  36.0 0.0 copy-start.4
  36.0 0.1 collective-permute-start.6
  36.0 0.1 collective-permute-start.5
  36.2 2.0 %collective-permute-start.4 = (f32[64,512]{1,0:T(8,128)S(1)}, f32[64,512]{1,0:T(8,128)S(1)}, u32[]{:S(2)}, u32[]{:S(2)}) collective-permute-start(f32[64,512]{1,0:T(8,128)S(1)} %broadcast_select_fusion.5.refs_0_), channel_id=1, source_target_pairs={{0,4},{2,6},{4,0},{6,2},{8,12},{10,14},{12,8},{14,10},{16,20},{18,... | collective-permute-start | bytes 393224 | tf_op jit(solution)/shard_map/ppermute | solution.py:310
  38.2 3.6 %collective-permute-done.6.refs_3_ = f32[64,512]{1,0:T(8,128)S(1)} collective-permute-done((f32[64,512]{1,0:T(8,128)S(1)}, f32[64,512]{1,0:T(8,128)S(1)}, u32[]{:S(2)}, u32[]{:S(2)}) %collective-permute-start.6) | collective-permute-done | bytes 131104 | tf_op jit(solution)/shard_map/ppermute | solution.py:310
  41.8 0.0 copy-start.8
  41.8 0.0 collective-permute-done.5.refs_2_
  41.8 0.0 copy-start.9
  41.8 1.1 %collective-permute-done.4.refs_1_ = f32[64,512]{1,0:T(8,128)S(1)} collective-permute-done((f32[64,512]{1,0:T(8,128)S(1)}, f32[64,512]{1,0:T(8,128)S(1)}, u32[]{:S(2)}, u32[]{:S(2)}) %collective-permute-start.4) | collective-permute-done | bytes 131104 | tf_op jit(solution)/shard_map/ppermute | solution.py:310
  42.9 0.0 copy-start.10
  42.9 0.0 copy-done.4
  43.0 0.0 copy-done.8
  43.0 0.0 copy-done.9
  43.0 0.6 copy-done.10
  43.6 8.6 %solve_upper.1 = (f32[128,512]{1,0:T(8,128)}, f32[128,512]{1,0:T(8,128)}, f32[256,512]{1,0:T(8,128)}) custom-call(s32[32]{0:T(128)} %slots.5, s32[1]{0:T(128)} %bitcast.me, f32[512,512]{1,0:T(8,128)} %s_ref.5, f32[512,512]{1,0:T(8,128)} %t_ref.5, f32[512,512]{1,0:T(8,128)} %r_ref.5, f32[1,512]{1,0:T(1,128)} %get-tuple-element.12.alpha_ref, ...), custom_call_target="tpu_custom_call" | custom-call | flops 1000 | bytes 1000 | tf_op jit(solution)/shard_map/solve_upper/pallas_call | solution.py:182
  52.2 1.1 collective-permute-start.7
  55.2 0.0 collective-permute-done.7
  55.3 0.7 collective-permute-start.8
  56.0 4.7 %collective-permute-done.8 = f32[64,512]{1,0:T(8,128)S(1)} collective-permute-done((f32[64,512]{1,0:T(8,128)S(1)}, f32[64,512]{1,0:T(8,128)S(1)}, u32[]{:S(2)}, u32[]{:S(2)}) %collective-permute-start.8) | collective-permute-done | bytes 131104 | tf_op jit(solution)/shard_map/ppermute | solution.py:310
  60.8 0.6 collective-permute-start.9
  61.4 4.5 %collective-permute-done.9 = f32[64,512]{1,0:T(8,128)S(1)} collective-permute-done((f32[64,512]{1,0:T(8,128)S(1)}, f32[64,512]{1,0:T(8,128)S(1)}, u32[]{:S(2)}, u32[]{:S(2)}) %collective-permute-start.9) | collective-permute-done | bytes 131104 | tf_op jit(solution)/shard_map/ppermute | solution.py:310
  65.8 2.1 %collective-permute-start.10 = (f32[64,512]{1,0:T(8,128)S(1)}, f32[64,512]{1,0:T(8,128)S(1)}, u32[]{:S(2)}, u32[]{:S(2)}) collective-permute-start(f32[64,512]{1,0:T(8,128)S(1)} %broadcast_select_fusion.2), channel_id=1, source_target_pairs={{0,16},{2,18},{4,20},{6,22},{8,24},{10,26},{12,28},{14,30},{16,0},... | collective-permute-start | bytes 393224 | tf_op jit(solution)/shard_map/ppermute | solution.py:310
  68.0 5.7 %collective-permute-done.10 = f32[64,512]{1,0:T(8,128)S(1)} collective-permute-done((f32[64,512]{1,0:T(8,128)S(1)}, f32[64,512]{1,0:T(8,128)S(1)}, u32[]{:S(2)}, u32[]{:S(2)}) %collective-permute-start.10) | collective-permute-done | bytes 131104 | tf_op jit(solution)/shard_map/ppermute | solution.py:310
  73.7 0.0 copy-start.3
  73.7 1.3 %collective-permute-start.13 = (f32[64,512]{1,0:T(8,128)S(1)}, f32[64,512]{1,0:T(8,128)S(1)}, u32[]{:S(2)}, u32[]{:S(2)}) collective-permute-start(f32[64,512]{1,0:T(8,128)S(1)} %broadcast_select_fusion.3.refs_0_), channel_id=1, source_target_pairs={{0,6},{2,4},{4,2},{6,0},{8,14},{10,12},{12,10},{14,8},{16,22},{18,... | collective-permute-start | bytes 393224 | tf_op jit(solution)/shard_map/ppermute | solution.py:310
  74.9 0.7 collective-permute-start.12
  75.6 0.2 collective-permute-start.11
  75.9 0.6 pad_add_fusion.parts
  76.5 2.7 %collective-permute-done.13.refs_3_ = f32[64,512]{1,0:T(8,128)S(1)} collective-permute-done((f32[64,512]{1,0:T(8,128)S(1)}, f32[64,512]{1,0:T(8,128)S(1)}, u32[]{:S(2)}, u32[]{:S(2)}) %collective-permute-start.13) | collective-permute-done | bytes 131104 | tf_op jit(solution)/shard_map/ppermute | solution.py:310
  79.3 0.0 copy-start.5
  79.3 0.0 collective-permute-done.12.refs_2_
  79.3 0.0 copy-start.6
  79.3 3.1 %collective-permute-done.11.refs_1_ = f32[64,512]{1,0:T(8,128)S(1)} collective-permute-done((f32[64,512]{1,0:T(8,128)S(1)}, f32[64,512]{1,0:T(8,128)S(1)}, u32[]{:S(2)}, u32[]{:S(2)}) %collective-permute-start.11) | collective-permute-done | bytes 131104 | tf_op jit(solution)/shard_map/ppermute | solution.py:310
  82.3 0.0 copy-start.7
  82.3 0.0 copy-done.3
  82.3 0.0 copy-done.5
  82.3 0.0 copy-done.6
  82.4 0.6 copy-done.7
  83.0 5.6 %finish_sides.1 = (f32[512,512]{1,0:T(8,128)}, bf16[768,512]{1,0:T(8,128)(2,1)}, bf16[768,512]{1,0:T(8,128)(2,1)}) custom-call(s32[32]{0:T(128)} %slots.5, s32[1]{0:T(128)} %bitcast.me, s32[2]{0:T(128)} %pad_add_fusion.parts, f32[512,512]{1,0:T(8,128)} %r_ref.5, f32[512,512]{1,0:T(8,128)} %s_ref.5, f32[512,512]{1,0:T(8,128)} %t_ref.5, ...), custom_call_target="tpu_custom_call" | custom-call | flops 1000 | bytes 1000 | tf_op jit(solution)/shard_map/finish_sides/pallas_call | solution.py:247
  88.6 0.0 copy-start
  88.6 2.2 %copy-done = f32[4096,2,128]{2,1,0:T(2,128)S(1)} copy-done((f32[4096,2,128]{2,1,0:T(2,128)S(1)}, f32[4096,2,128]{2,1,0:T(2,128)}, u32[]{:S(2)}) %copy-start) | copy-done | bytes 4194328
  90.8 0.0 copy-start.2
  90.8 1.1 %copy-done.2 = bf16[768,512]{1,0:T(8,128)(2,1)S(1)} copy-done((bf16[768,512]{1,0:T(8,128)(2,1)S(1)}, bf16[768,512]{1,0:T(8,128)(2,1)}, u32[]{:S(2)}) %copy-start.2) | copy-done | bytes 786456
  91.9 0.0 copy-start.1
  91.9 8.1 %add_own.1.base_ref = f32[4096,512]{1,0:T(8,128)S(1)} custom-call(f32[4096,512]{1,0:T(8,128)} %base_ref.1, bf16[768,512]{1,0:T(8,128)(2,1)S(1)} %copy-done.2, f32[8192,128]{1,0:T(8,128)S(1)} %bitcast.10), custom_call_target="tpu_custom_call" | custom-call | flops 1000 | bytes 1000 | tf_op jit(solution)/shard_map/add_own/pallas_call | solution.py:283
  100.1 0.0 collective-permute-done.14.refs_0_
  100.1 0.0 copy-done.1
  100.1 9.3 %add_received.1 = f32[4096,512]{1,0:T(8,128)} custom-call(f32[4096,512]{1,0:T(8,128)S(1)} %add_own.1.base_ref, bf16[768,512]{1,0:T(8,128)(2,1)S(1)} %copy-done.1, f32[8192,128]{1,0:T(8,128)} %collective-permute-done.14.refs_0_), custom_call_target="tpu_custom_call" | custom-call | flops 1000 | bytes 1000 | tf_op jit(solution)/shard_map/add_received/pallas_call | solution.py:283
  (10 shorter events, 0.3 us)
Async XLA Ops:
  0.6 99.4 %collective-permute-start.14 = (f32[8192,128]{1,0:T(8,128)}, f32[8192,128]{1,0:T(8,128)}, u32[]{:S(2)}, u32[]{:S(2)}) collective-permute-start(f32[8192,128]{1,0:T(8,128)} %bitcast.9), channel_id=1, source_target_pairs={{0,1},{1,0},{2,3},{3,2},{4,5},{5,4},{6,7},{7,6},{8,9},{9,8},{10,11... | collective-permute-start | bytes 12582920 | tf_op jit(solution)/shard_map/ppermute | solution.py:350
  11.4 3.5 %collective-permute-start = (f32[128,512]{1,0:T(8,128)}, f32[128,512]{1,0:T(8,128)S(1)}, u32[]{:S(2)}, u32[]{:S(2)}) collective-permute-start(f32[128,512]{1,0:T(8,128)} %get-tuple-element.15), channel_id=1, source_target_pairs={{0,2},{2,0},{4,6},{6,4},{8,10},{10,8},{12,14},{14,12},{16,18},{18,... | collective-permute-start | bytes 786440 | tf_op jit(solution)/shard_map/ppermute | solution.py:310
  14.9 6.0 %collective-permute-start.1 = (f32[64,512]{1,0:T(8,128)S(1)}, f32[64,512]{1,0:T(8,128)S(1)}, u32[]{:S(2)}, u32[]{:S(2)}) collective-permute-start(f32[64,512]{1,0:T(8,128)S(1)} %slice_select_fusion.1), channel_id=1, source_target_pairs={{0,4},{2,6},{4,0},{6,2},{8,12},{10,14},{12,8},{14,10},{16,20},{18,... | collective-permute-start | bytes 393224 | tf_op jit(solution)/shard_map/ppermute | solution.py:310
  20.9 6.0 %collective-permute-start.2 = (f32[64,512]{1,0:T(8,128)S(1)}, f32[64,512]{1,0:T(8,128)S(1)}, u32[]{:S(2)}, u32[]{:S(2)}) collective-permute-start(f32[64,512]{1,0:T(8,128)S(1)} %select_select_fusion.1), channel_id=1, source_target_pairs={{0,8},{2,10},{4,12},{6,14},{8,0},{10,2},{12,4},{14,6},{16,24},{18,... | collective-permute-start | bytes 393224 | tf_op jit(solution)/shard_map/ppermute | solution.py:310
  26.9 9.0 %collective-permute-start.3 = (f32[64,512]{1,0:T(8,128)S(1)}, f32[64,512]{1,0:T(8,128)S(1)}, u32[]{:S(2)}, u32[]{:S(2)}) collective-permute-start(f32[64,512]{1,0:T(8,128)S(1)} %broadcast_select_fusion.4), channel_id=1, source_target_pairs={{0,16},{2,18},{4,20},{6,22},{8,24},{10,26},{12,28},{14,30},{16,0},... | collective-permute-start | bytes 393224 | tf_op jit(solution)/shard_map/ppermute | solution.py:310
  36.0 7.0 %copy-start.4 = (f32[64,512]{1,0:T(8,128)}, f32[64,512]{1,0:T(8,128)S(1)}, u32[]{:S(2)}) copy-start(f32[64,512]{1,0:T(8,128)S(1)} %broadcast_select_fusion.5.refs_0_) | copy-start | bytes 393220
  36.0 5.8 %collective-permute-start.6 = (f32[64,512]{1,0:T(8,128)S(1)}, f32[64,512]{1,0:T(8,128)S(1)}, u32[]{:S(2)}, u32[]{:S(2)}) collective-permute-start(f32[64,512]{1,0:T(8,128)S(1)} %broadcast_select_fusion.5.refs_0_), channel_id=1, source_target_pairs={{0,6},{2,4},{4,2},{6,0},{8,14},{10,12},{12,10},{14,8},{16,22},{18,... | collective-permute-start | bytes 393224 | tf_op jit(solution)/shard_map/ppermute | solution.py:310
  36.0 5.8 %collective-permute-start.5 = (f32[64,512]{1,0:T(8,128)S(1)}, f32[64,512]{1,0:T(8,128)S(1)}, u32[]{:S(2)}, u32[]{:S(2)}) collective-permute-start(f32[64,512]{1,0:T(8,128)S(1)} %broadcast_select_fusion.5.refs_0_), channel_id=1, source_target_pairs={{0,2},{2,0},{4,6},{6,4},{8,10},{10,8},{12,14},{14,12},{16,18},{18,... | collective-permute-start | bytes 393224 | tf_op jit(solution)/shard_map/ppermute | solution.py:310
  36.2 6.8 %collective-permute-start.4 = (f32[64,512]{1,0:T(8,128)S(1)}, f32[64,512]{1,0:T(8,128)S(1)}, u32[]{:S(2)}, u32[]{:S(2)}) collective-permute-start(f32[64,512]{1,0:T(8,128)S(1)} %broadcast_select_fusion.5.refs_0_), channel_id=1, source_target_pairs={{0,4},{2,6},{4,0},{6,2},{8,12},{10,14},{12,8},{14,10},{16,20},{18,... | collective-permute-start | bytes 393224 | tf_op jit(solution)/shard_map/ppermute | solution.py:310
  41.8 1.2 %copy-start.8 = (f32[64,512]{1,0:T(8,128)}, f32[64,512]{1,0:T(8,128)S(1)}, u32[]{:S(2)}) copy-start(f32[64,512]{1,0:T(8,128)S(1)} %collective-permute-done.6.refs_3_) | copy-start | bytes 393220
  41.8 1.2 %copy-start.9 = (f32[64,512]{1,0:T(8,128)}, f32[64,512]{1,0:T(8,128)S(1)}, u32[]{:S(2)}) copy-start(f32[64,512]{1,0:T(8,128)S(1)} %collective-permute-done.5.refs_2_) | copy-start | bytes 393220
  42.9 0.6 copy-start.10
  52.2 3.0 %collective-permute-start.7 = (f32[128,512]{1,0:T(8,128)}, f32[128,512]{1,0:T(8,128)S(1)}, u32[]{:S(2)}, u32[]{:S(2)}) collective-permute-start(f32[128,512]{1,0:T(8,128)} %get-tuple-element.18), channel_id=1, source_target_pairs={{0,2},{2,0},{4,6},{6,4},{8,10},{10,8},{12,14},{14,12},{16,18},{18,... | collective-permute-start | bytes 786440 | tf_op jit(solution)/shard_map/ppermute | solution.py:310
  55.3 5.5 %collective-permute-start.8 = (f32[64,512]{1,0:T(8,128)S(1)}, f32[64,512]{1,0:T(8,128)S(1)}, u32[]{:S(2)}, u32[]{:S(2)}) collective-permute-start(f32[64,512]{1,0:T(8,128)S(1)} %slice_select_fusion), channel_id=1, source_target_pairs={{0,4},{2,6},{4,0},{6,2},{8,12},{10,14},{12,8},{14,10},{16,20},{18,... | collective-permute-start | bytes 393224 | tf_op jit(solution)/shard_map/ppermute | solution.py:310
  60.8 5.0 %collective-permute-start.9 = (f32[64,512]{1,0:T(8,128)S(1)}, f32[64,512]{1,0:T(8,128)S(1)}, u32[]{:S(2)}, u32[]{:S(2)}) collective-permute-start(f32[64,512]{1,0:T(8,128)S(1)} %select_select_fusion), channel_id=1, source_target_pairs={{0,8},{2,10},{4,12},{6,14},{8,0},{10,2},{12,4},{14,6},{16,24},{18,... | collective-permute-start | bytes 393224 | tf_op jit(solution)/shard_map/ppermute | solution.py:310
  65.8 7.8 %collective-permute-start.10 = (f32[64,512]{1,0:T(8,128)S(1)}, f32[64,512]{1,0:T(8,128)S(1)}, u32[]{:S(2)}, u32[]{:S(2)}) collective-permute-start(f32[64,512]{1,0:T(8,128)S(1)} %broadcast_select_fusion.2), channel_id=1, source_target_pairs={{0,16},{2,18},{4,20},{6,22},{8,24},{10,26},{12,28},{14,30},{16,0},... | collective-permute-start | bytes 393224 | tf_op jit(solution)/shard_map/ppermute | solution.py:310
  73.7 8.7 %copy-start.3 = (f32[64,512]{1,0:T(8,128)}, f32[64,512]{1,0:T(8,128)S(1)}, u32[]{:S(2)}) copy-start(f32[64,512]{1,0:T(8,128)S(1)} %broadcast_select_fusion.3.refs_0_) | copy-start | bytes 393220
  73.7 5.6 %collective-permute-start.13 = (f32[64,512]{1,0:T(8,128)S(1)}, f32[64,512]{1,0:T(8,128)S(1)}, u32[]{:S(2)}, u32[]{:S(2)}) collective-permute-start(f32[64,512]{1,0:T(8,128)S(1)} %broadcast_select_fusion.3.refs_0_), channel_id=1, source_target_pairs={{0,6},{2,4},{4,2},{6,0},{8,14},{10,12},{12,10},{14,8},{16,22},{18,... | collective-permute-start | bytes 393224 | tf_op jit(solution)/shard_map/ppermute | solution.py:310
  74.9 4.4 %collective-permute-start.12 = (f32[64,512]{1,0:T(8,128)S(1)}, f32[64,512]{1,0:T(8,128)S(1)}, u32[]{:S(2)}, u32[]{:S(2)}) collective-permute-start(f32[64,512]{1,0:T(8,128)S(1)} %broadcast_select_fusion.3.refs_0_), channel_id=1, source_target_pairs={{0,2},{2,0},{4,6},{6,4},{8,10},{10,8},{12,14},{14,12},{16,18},{18,... | collective-permute-start | bytes 393224 | tf_op jit(solution)/shard_map/ppermute | solution.py:310
  75.6 6.7 %collective-permute-start.11 = (f32[64,512]{1,0:T(8,128)S(1)}, f32[64,512]{1,0:T(8,128)S(1)}, u32[]{:S(2)}, u32[]{:S(2)}) collective-permute-start(f32[64,512]{1,0:T(8,128)S(1)} %broadcast_select_fusion.3.refs_0_), channel_id=1, source_target_pairs={{0,4},{2,6},{4,0},{6,2},{8,12},{10,14},{12,8},{14,10},{16,20},{18,... | collective-permute-start | bytes 393224 | tf_op jit(solution)/shard_map/ppermute | solution.py:310
  79.3 3.1 %copy-start.5 = (f32[64,512]{1,0:T(8,128)}, f32[64,512]{1,0:T(8,128)S(1)}, u32[]{:S(2)}) copy-start(f32[64,512]{1,0:T(8,128)S(1)} %collective-permute-done.13.refs_3_) | copy-start | bytes 393220
  79.3 3.1 %copy-start.6 = (f32[64,512]{1,0:T(8,128)}, f32[64,512]{1,0:T(8,128)S(1)}, u32[]{:S(2)}) copy-start(f32[64,512]{1,0:T(8,128)S(1)} %collective-permute-done.12.refs_2_) | copy-start | bytes 393220
  82.3 0.7 copy-start.7
  88.6 2.2 %copy-start = (f32[4096,2,128]{2,1,0:T(2,128)S(1)}, f32[4096,2,128]{2,1,0:T(2,128)}, u32[]{:S(2)}) copy-start(f32[4096,2,128]{2,1,0:T(2,128)} %param.16) | copy-start | bytes 12582916
  90.8 1.1 %copy-start.2 = (bf16[768,512]{1,0:T(8,128)(2,1)S(1)}, bf16[768,512]{1,0:T(8,128)(2,1)}, u32[]{:S(2)}) copy-start(bf16[768,512]{1,0:T(8,128)(2,1)} %get-tuple-element.20.terms_ref) | copy-start | bytes 2359300
  91.9 8.1 %copy-start.1 = (bf16[768,512]{1,0:T(8,128)(2,1)S(1)}, bf16[768,512]{1,0:T(8,128)(2,1)}, u32[]{:S(2)}) copy-start(bf16[768,512]{1,0:T(8,128)(2,1)} %get-tuple-element.21.terms_ref) | copy-start | bytes 2359300

commit v2 on v1

--- a/solution.py
+++ b/solution.py
@@ -10,7 +10,7 @@
 
 SUB = 32
 GROUP = 8
-VMEM_BYTES = 57 * 1024 * 1024
+VMEM_BYTES = 109 * 512 * 1024
 ADD_VMEM_BYTES = 36 * 1024 * 1024
 FULL_VMEM_BYTES = 59 * 1024 * 1024
 TILE = 512

time: 110 us -> 112 us (1.018)
  starting transfers between devices: 17.1 us -> 18.6 us
    ppermute x14, starting transfers between devices: 14.1 us -> 15.6 us  [exchange(): return lax.ppermute(value, axis, [(i, i ^ bit) for i in range(size)])]
  transfers between devices with their start and end apart: 15 -> 15, of which waited for: 10 -> 10; matrix products, arithmetic and copies ran while one was open for 2% -> 2% of each run, Pallas kernels for 28% -> 27%
where the time goes in v2:
time: 112 us; the launch traced here: 111 us
  waiting for transfers between devices  41.6 us (37%)
  Pallas kernels  39.3 us (35%)
  starting transfers between devices  18.6 us (17%)
  local copies, waits for them, and re-layouts  6 us (5%)
  between operations  4.73 us (4%)
    ppermute x14, waiting for transfers between devices, exchange(): return lax.ppermute(value, axis, [(i, i ^ bit) for i in range(size)])  41.6 us
    pallas_call x2, Pallas kernels, add_product(): pl.pallas_call(functools.partial(add_kernel, paired, held), out_shape=jax...  17.4 us
    ppermute x14, starting transfers between devices, exchange(): return lax.ppermute(value, axis, [(i, i ^ bit) for i in range(size)])  15.6 us
    pallas_call x1, Pallas kernels, solve_upper(): pl.pallas_call(upper_kernel, out_shape=(*[jax.ShapeDtypeStruct((block //...  8.65 us
    pallas_call x1, Pallas kernels, solve_lower(): pl.pallas_call(lower_kernel, out_shape=(*[jax.ShapeDtypeStruct((block //...  7.7 us
    pallas_call x1, Pallas kernels, finish_sides(): pl.pallas_call(finish_kernel, out_shape=(jax.ShapeDtypeStruct(sides.shape...  5.61 us
    unnamed x22, local copies, waits for them, and re-layouts  4.62 us
    ppermute x1, starting transfers between devices, on_device(): lax.ppermute(own, 'col', [(i, (i + step) % col_size) for i in range(col_s...  3.03 us
  transfers between devices with their start and end apart: 15, of which 10 were waited for; matrix products, arithmetic and copies ran while one was open for 2% of the time, Pallas kernels for 27%

profile of v2, /device:TPU:0, one launch (start us, length us, event | category | flops | bytes accessed | tf_op | source)
XLA Modules:
  0.0 111.2 jit_solution(18428819492078268564)
XLA Ops:
  0.6 3.0 %collective-permute-start.14 = (f32[8192,128]{1,0:T(8,128)}, f32[8192,128]{1,0:T(8,128)}, u32[]{:S(2)}, u32[]{:S(2)}) collective-permute-start(f32[8192,128]{1,0:T(8,128)} %bitcast.9), channel_id=1, source_target_pairs={{0,1},{1,0},{2,3},{3,2},{4,5},{5,4},{6,7},{7,6},{8,9},{9,8},{10,11... | collective-permute-start | bytes 12582920 | tf_op jit(solution)/shard_map/ppermute | solution.py:350
  3.7 7.7 %solve_lower.1 = (f32[128,512]{1,0:T(8,128)}, f32[128,512]{1,0:T(8,128)}, f32[1,512]{1,0:T(1,128)}, f32[1,512]{1,0:T(1,128)}) custom-call(s32[32]{0:T(128)} %slots.5, s32[1]{0:T(128)} %bitcast.me, f32[512,512]{1,0:T(8,128)} %s_ref.5, f32[512,512]{1,0:T(8,128)} %t_ref.5, f32[512,512]{1,0:T(8,128)} %r_ref.5, f32[32,128]{1,0:T(8,128)} %bitcast.11, ...), custom_call_target="tpu_custom_call" | custom-call | flops 1000 | bytes 1000 | tf_op jit(solution)/shard_map/solve_lower/pallas_call | solution.py:146
  11.4 0.0 collective-permute-start
  11.4 1.4 %fusion = (s32[1]{0:T(128)}, s32[1]{0:T(128)}) fusion(s32[32]{0:T(128)} %slots.5), kind=kLoop, calls=%fused_computation.11 | loop fusion | bytes 16 | tf_op jit(solution)/shard_map/slice | solution.py:344
  14.8 0.0 collective-permute-done
  14.9 1.6 %collective-permute-start.1 = (f32[64,512]{1,0:T(8,128)S(1)}, f32[64,512]{1,0:T(8,128)S(1)}, u32[]{:S(2)}, u32[]{:S(2)}) collective-permute-start(f32[64,512]{1,0:T(8,128)S(1)} %slice_select_fusion.1), channel_id=1, source_target_pairs={{0,4},{2,6},{4,0},{6,2},{8,12},{10,14},{12,8},{14,10},{16,20},{18,... | collective-permute-start | bytes 393224 | tf_op jit(solution)/shard_map/ppermute | solution.py:310
  16.5 4.4 %collective-permute-done.1 = f32[64,512]{1,0:T(8,128)S(1)} collective-permute-done((f32[64,512]{1,0:T(8,128)S(1)}, f32[64,512]{1,0:T(8,128)S(1)}, u32[]{:S(2)}, u32[]{:S(2)}) %collective-permute-start.1) | collective-permute-done | bytes 131104 | tf_op jit(solution)/shard_map/ppermute | solution.py:310
  20.9 1.6 %collective-permute-start.2 = (f32[64,512]{1,0:T(8,128)S(1)}, f32[64,512]{1,0:T(8,128)S(1)}, u32[]{:S(2)}, u32[]{:S(2)}) collective-permute-start(f32[64,512]{1,0:T(8,128)S(1)} %select_select_fusion.1), channel_id=1, source_target_pairs={{0,8},{2,10},{4,12},{6,14},{8,0},{10,2},{12,4},{14,6},{16,24},{18,... | collective-permute-start | bytes 393224 | tf_op jit(solution)/shard_map/ppermute | solution.py:310
  22.5 3.7 %collective-permute-done.2 = f32[64,512]{1,0:T(8,128)S(1)} collective-permute-done((f32[64,512]{1,0:T(8,128)S(1)}, f32[64,512]{1,0:T(8,128)S(1)}, u32[]{:S(2)}, u32[]{:S(2)}) %collective-permute-start.2) | collective-permute-done | bytes 131104 | tf_op jit(solution)/shard_map/ppermute | solution.py:310
  26.2 3.3 %collective-permute-start.3 = (f32[64,512]{1,0:T(8,128)S(1)}, f32[64,512]{1,0:T(8,128)S(1)}, u32[]{:S(2)}, u32[]{:S(2)}) collective-permute-start(f32[64,512]{1,0:T(8,128)S(1)} %broadcast_select_fusion.4), channel_id=1, source_target_pairs={{0,16},{2,18},{4,20},{6,22},{8,24},{10,26},{12,28},{14,30},{16,0},... | collective-permute-start | bytes 393224 | tf_op jit(solution)/shard_map/ppermute | solution.py:310
  29.6 6.3 %collective-permute-done.3 = f32[64,512]{1,0:T(8,128)S(1)} collective-permute-done((f32[64,512]{1,0:T(8,128)S(1)}, f32[64,512]{1,0:T(8,128)S(1)}, u32[]{:S(2)}, u32[]{:S(2)}) %collective-permute-start.3) | collective-permute-done | bytes 131104 | tf_op jit(solution)/shard_map/ppermute | solution.py:310
  35.9 0.0 copy-start.4
  35.9 0.4 collective-permute-start.6
  36.4 1.2 %collective-permute-start.5 = (f32[64,512]{1,0:T(8,128)S(1)}, f32[64,512]{1,0:T(8,128)S(1)}, u32[]{:S(2)}, u32[]{:S(2)}) collective-permute-start(f32[64,512]{1,0:T(8,128)S(1)} %broadcast_select_fusion.5.refs_0_), channel_id=1, source_target_pairs={{0,2},{2,0},{4,6},{6,4},{8,10},{10,8},{12,14},{14,12},{16,18},{18,... | collective-permute-start | bytes 393224 | tf_op jit(solution)/shard_map/ppermute | solution.py:310
  37.6 0.5 collective-permute-start.4
  38.1 3.6 %collective-permute-done.6.refs_3_ = f32[64,512]{1,0:T(8,128)S(1)} collective-permute-done((f32[64,512]{1,0:T(8,128)S(1)}, f32[64,512]{1,0:T(8,128)S(1)}, u32[]{:S(2)}, u32[]{:S(2)}) %collective-permute-start.6) | collective-permute-done | bytes 131104 | tf_op jit(solution)/shard_map/ppermute | solution.py:310
  41.7 0.0 copy-start.8
  41.7 0.0 collective-permute-done.5.refs_2_
  41.7 0.0 copy-start.9
  41.8 2.8 %collective-permute-done.4.refs_1_ = f32[64,512]{1,0:T(8,128)S(1)} collective-permute-done((f32[64,512]{1,0:T(8,128)S(1)}, f32[64,512]{1,0:T(8,128)S(1)}, u32[]{:S(2)}, u32[]{:S(2)}) %collective-permute-start.4) | collective-permute-done | bytes 131104 | tf_op jit(solution)/shard_map/ppermute | solution.py:310
  44.6 0.0 copy-start.10
  44.6 0.0 copy-done.4
  44.6 0.0 copy-done.8
  44.6 0.0 copy-done.9
  44.6 0.6 copy-done.10
  45.2 8.6 %solve_upper.1 = (f32[128,512]{1,0:T(8,128)}, f32[128,512]{1,0:T(8,128)}, f32[256,512]{1,0:T(8,128)}) custom-call(s32[32]{0:T(128)} %slots.5, s32[1]{0:T(128)} %bitcast.me, f32[512,512]{1,0:T(8,128)} %s_ref.5, f32[512,512]{1,0:T(8,128)} %t_ref.5, f32[512,512]{1,0:T(8,128)} %r_ref.5, f32[1,512]{1,0:T(1,128)} %get-tuple-element.12.alpha_ref, ...), custom_call_target="tpu_custom_call" | custom-call | flops 1000 | bytes 1000 | tf_op jit(solution)/shard_map/solve_upper/pallas_call | solution.py:182
  53.9 0.2 collective-permute-start.7
  56.0 0.0 collective-permute-done.7
  56.0 1.1 collective-permute-start.8
  57.1 4.7 %collective-permute-done.8 = f32[64,512]{1,0:T(8,128)S(1)} collective-permute-done((f32[64,512]{1,0:T(8,128)S(1)}, f32[64,512]{1,0:T(8,128)S(1)}, u32[]{:S(2)}, u32[]{:S(2)}) %collective-permute-start.8) | collective-permute-done | bytes 131104 | tf_op jit(solution)/shard_map/ppermute | solution.py:310
  61.9 0.8 collective-permute-start.9
  62.7 4.3 %collective-permute-done.9 = f32[64,512]{1,0:T(8,128)S(1)} collective-permute-done((f32[64,512]{1,0:T(8,128)S(1)}, f32[64,512]{1,0:T(8,128)S(1)}, u32[]{:S(2)}, u32[]{:S(2)}) %collective-permute-start.9) | collective-permute-done | bytes 131104 | tf_op jit(solution)/shard_map/ppermute | solution.py:310
  67.0 2.6 %collective-permute-start.10 = (f32[64,512]{1,0:T(8,128)S(1)}, f32[64,512]{1,0:T(8,128)S(1)}, u32[]{:S(2)}, u32[]{:S(2)}) collective-permute-start(f32[64,512]{1,0:T(8,128)S(1)} %broadcast_select_fusion.2), channel_id=1, source_target_pairs={{0,16},{2,18},{4,20},{6,22},{8,24},{10,26},{12,28},{14,30},{16,0},... | collective-permute-start | bytes 393224 | tf_op jit(solution)/shard_map/ppermute | solution.py:310
  69.6 5.8 %collective-permute-done.10 = f32[64,512]{1,0:T(8,128)S(1)} collective-permute-done((f32[64,512]{1,0:T(8,128)S(1)}, f32[64,512]{1,0:T(8,128)S(1)}, u32[]{:S(2)}, u32[]{:S(2)}) %collective-permute-start.10) | collective-permute-done | bytes 131104 | tf_op jit(solution)/shard_map/ppermute | solution.py:310
  75.5 0.0 copy-start.3
  75.5 0.3 collective-permute-start.13
  75.8 1.4 %collective-permute-start.12 = (f32[64,512]{1,0:T(8,128)S(1)}, f32[64,512]{1,0:T(8,128)S(1)}, u32[]{:S(2)}, u32[]{:S(2)}) collective-permute-start(f32[64,512]{1,0:T(8,128)S(1)} %broadcast_select_fusion.3.refs_0_), channel_id=1, source_target_pairs={{0,2},{2,0},{4,6},{6,4},{8,10},{10,8},{12,14},{14,12},{16,18},{18,... | collective-permute-start | bytes 393224 | tf_op jit(solution)/shard_map/ppermute | solution.py:310
  77.2 0.5 collective-permute-start.11
  77.7 0.6 pad_add_fusion.parts
  78.3 3.0 %collective-permute-done.13.refs_3_ = f32[64,512]{1,0:T(8,128)S(1)} collective-permute-done((f32[64,512]{1,0:T(8,128)S(1)}, f32[64,512]{1,0:T(8,128)S(1)}, u32[]{:S(2)}, u32[]{:S(2)}) %collective-permute-start.13) | collective-permute-done | bytes 131104 | tf_op jit(solution)/shard_map/ppermute | solution.py:310
  81.3 0.0 copy-start.5
  81.3 0.0 collective-permute-done.12.refs_2_
  81.3 0.0 copy-start.6
  81.3 2.8 %collective-permute-done.11.refs_1_ = f32[64,512]{1,0:T(8,128)S(1)} collective-permute-done((f32[64,512]{1,0:T(8,128)S(1)}, f32[64,512]{1,0:T(8,128)S(1)}, u32[]{:S(2)}, u32[]{:S(2)}) %collective-permute-start.11) | collective-permute-done | bytes 131104 | tf_op jit(solution)/shard_map/ppermute | solution.py:310
  84.2 0.0 copy-start.7
  84.2 0.0 copy-done.3
  84.2 0.0 copy-done.5
  84.2 0.0 copy-done.6
  84.2 0.6 copy-done.7
  84.8 5.6 %finish_sides.1 = (f32[512,512]{1,0:T(8,128)}, bf16[768,512]{1,0:T(8,128)(2,1)}, bf16[768,512]{1,0:T(8,128)(2,1)}) custom-call(s32[32]{0:T(128)} %slots.5, s32[1]{0:T(128)} %bitcast.me, s32[2]{0:T(128)} %pad_add_fusion.parts, f32[512,512]{1,0:T(8,128)} %r_ref.5, f32[512,512]{1,0:T(8,128)} %s_ref.5, f32[512,512]{1,0:T(8,128)} %t_ref.5, ...), custom_call_target="tpu_custom_call" | custom-call | flops 1000 | bytes 1000 | tf_op jit(solution)/shard_map/finish_sides/pallas_call | solution.py:247
  90.4 0.0 copy-start
  90.4 2.2 %copy-done = f32[4096,2,128]{2,1,0:T(2,128)S(1)} copy-done((f32[4096,2,128]{2,1,0:T(2,128)S(1)}, f32[4096,2,128]{2,1,0:T(2,128)}, u32[]{:S(2)}) %copy-start) | copy-done | bytes 4194328
  92.6 0.0 copy-start.2
  92.6 1.1 %copy-done.2 = bf16[768,512]{1,0:T(8,128)(2,1)S(1)} copy-done((bf16[768,512]{1,0:T(8,128)(2,1)S(1)}, bf16[768,512]{1,0:T(8,128)(2,1)}, u32[]{:S(2)}) %copy-start.2) | copy-done | bytes 786456
  93.7 0.0 copy-start.1
  93.8 8.1 %add_own.1.base_ref = f32[4096,512]{1,0:T(8,128)S(1)} custom-call(f32[4096,512]{1,0:T(8,128)} %base_ref.1, bf16[768,512]{1,0:T(8,128)(2,1)S(1)} %copy-done.2, f32[8192,128]{1,0:T(8,128)S(1)} %bitcast.10), custom_call_target="tpu_custom_call" | custom-call | flops 1000 | bytes 1000 | tf_op jit(solution)/shard_map/add_own/pallas_call | solution.py:283
  101.9 0.0 collective-permute-done.14.refs_0_
  101.9 0.0 copy-done.1
  101.9 9.3 %add_received.1 = f32[4096,512]{1,0:T(8,128)} custom-call(f32[4096,512]{1,0:T(8,128)S(1)} %add_own.1.base_ref, bf16[768,512]{1,0:T(8,128)(2,1)S(1)} %copy-done.1, f32[8192,128]{1,0:T(8,128)} %collective-permute-done.14.refs_0_), custom_call_target="tpu_custom_call" | custom-call | flops 1000 | bytes 1000 | tf_op jit(solution)/shard_map/add_received/pallas_call | solution.py:283
  (10 shorter events, 0.3 us)
Async XLA Ops:
  0.6 101.3 %collective-permute-start.14 = (f32[8192,128]{1,0:T(8,128)}, f32[8192,128]{1,0:T(8,128)}, u32[]{:S(2)}, u32[]{:S(2)}) collective-permute-start(f32[8192,128]{1,0:T(8,128)} %bitcast.9), channel_id=1, source_target_pairs={{0,1},{1,0},{2,3},{3,2},{4,5},{5,4},{6,7},{7,6},{8,9},{9,8},{10,11... | collective-permute-start | bytes 12582920 | tf_op jit(solution)/shard_map/ppermute | solution.py:350
  11.4 3.5 %collective-permute-start = (f32[128,512]{1,0:T(8,128)}, f32[128,512]{1,0:T(8,128)S(1)}, u32[]{:S(2)}, u32[]{:S(2)}) collective-permute-start(f32[128,512]{1,0:T(8,128)} %get-tuple-element.15), channel_id=1, source_target_pairs={{0,2},{2,0},{4,6},{6,4},{8,10},{10,8},{12,14},{14,12},{16,18},{18,... | collective-permute-start | bytes 786440 | tf_op jit(solution)/shard_map/ppermute | solution.py:310
  14.9 6.0 %collective-permute-start.1 = (f32[64,512]{1,0:T(8,128)S(1)}, f32[64,512]{1,0:T(8,128)S(1)}, u32[]{:S(2)}, u32[]{:S(2)}) collective-permute-start(f32[64,512]{1,0:T(8,128)S(1)} %slice_select_fusion.1), channel_id=1, source_target_pairs={{0,4},{2,6},{4,0},{6,2},{8,12},{10,14},{12,8},{14,10},{16,20},{18,... | collective-permute-start | bytes 393224 | tf_op jit(solution)/shard_map/ppermute | solution.py:310
  20.9 5.3 %collective-permute-start.2 = (f32[64,512]{1,0:T(8,128)S(1)}, f32[64,512]{1,0:T(8,128)S(1)}, u32[]{:S(2)}, u32[]{:S(2)}) collective-permute-start(f32[64,512]{1,0:T(8,128)S(1)} %select_select_fusion.1), channel_id=1, source_target_pairs={{0,8},{2,10},{4,12},{6,14},{8,0},{10,2},{12,4},{14,6},{16,24},{18,... | collective-permute-start | bytes 393224 | tf_op jit(solution)/shard_map/ppermute | solution.py:310
  26.2 9.7 %collective-permute-start.3 = (f32[64,512]{1,0:T(8,128)S(1)}, f32[64,512]{1,0:T(8,128)S(1)}, u32[]{:S(2)}, u32[]{:S(2)}) collective-permute-start(f32[64,512]{1,0:T(8,128)S(1)} %broadcast_select_fusion.4), channel_id=1, source_target_pairs={{0,16},{2,18},{4,20},{6,22},{8,24},{10,26},{12,28},{14,30},{16,0},... | collective-permute-start | bytes 393224 | tf_op jit(solution)/shard_map/ppermute | solution.py:310
  35.9 8.7 %copy-start.4 = (f32[64,512]{1,0:T(8,128)}, f32[64,512]{1,0:T(8,128)S(1)}, u32[]{:S(2)}) copy-start(f32[64,512]{1,0:T(8,128)S(1)} %broadcast_select_fusion.5.refs_0_) | copy-start | bytes 393220
  35.9 5.8 %collective-permute-start.6 = (f32[64,512]{1,0:T(8,128)S(1)}, f32[64,512]{1,0:T(8,128)S(1)}, u32[]{:S(2)}, u32[]{:S(2)}) collective-permute-start(f32[64,512]{1,0:T(8,128)S(1)} %broadcast_select_fusion.5.refs_0_), channel_id=1, source_target_pairs={{0,6},{2,4},{4,2},{6,0},{8,14},{10,12},{12,10},{14,8},{16,22},{18,... | collective-permute-start | bytes 393224 | tf_op jit(solution)/shard_map/ppermute | solution.py:310
  36.4 5.4 %collective-permute-start.5 = (f32[64,512]{1,0:T(8,128)S(1)}, f32[64,512]{1,0:T(8,128)S(1)}, u32[]{:S(2)}, u32[]{:S(2)}) collective-permute-start(f32[64,512]{1,0:T(8,128)S(1)} %broadcast_select_fusion.5.refs_0_), channel_id=1, source_target_pairs={{0,2},{2,0},{4,6},{6,4},{8,10},{10,8},{12,14},{14,12},{16,18},{18,... | collective-permute-start | bytes 393224 | tf_op jit(solution)/shard_map/ppermute | solution.py:310
  37.6 7.0 %collective-permute-start.4 = (f32[64,512]{1,0:T(8,128)S(1)}, f32[64,512]{1,0:T(8,128)S(1)}, u32[]{:S(2)}, u32[]{:S(2)}) collective-permute-start(f32[64,512]{1,0:T(8,128)S(1)} %broadcast_select_fusion.5.refs_0_), channel_id=1, source_target_pairs={{0,4},{2,6},{4,0},{6,2},{8,12},{10,14},{12,8},{14,10},{16,20},{18,... | collective-permute-start | bytes 393224 | tf_op jit(solution)/shard_map/ppermute | solution.py:310
  41.7 2.9 %copy-start.8 = (f32[64,512]{1,0:T(8,128)}, f32[64,512]{1,0:T(8,128)S(1)}, u32[]{:S(2)}) copy-start(f32[64,512]{1,0:T(8,128)S(1)} %collective-permute-done.6.refs_3_) | copy-start | bytes 393220
  41.7 2.9 %copy-start.9 = (f32[64,512]{1,0:T(8,128)}, f32[64,512]{1,0:T(8,128)S(1)}, u32[]{:S(2)}) copy-start(f32[64,512]{1,0:T(8,128)S(1)} %collective-permute-done.5.refs_2_) | copy-start | bytes 393220
  44.6 0.6 copy-start.10
  53.9 2.1 %collective-permute-start.7 = (f32[128,512]{1,0:T(8,128)}, f32[128,512]{1,0:T(8,128)S(1)}, u32[]{:S(2)}, u32[]{:S(2)}) collective-permute-start(f32[128,512]{1,0:T(8,128)} %get-tuple-element.18), channel_id=1, source_target_pairs={{0,2},{2,0},{4,6},{6,4},{8,10},{10,8},{12,14},{14,12},{16,18},{18,... | collective-permute-start | bytes 786440 | tf_op jit(solution)/shard_map/ppermute | solution.py:310
  56.0 5.8 %collective-permute-start.8 = (f32[64,512]{1,0:T(8,128)S(1)}, f32[64,512]{1,0:T(8,128)S(1)}, u32[]{:S(2)}, u32[]{:S(2)}) collective-permute-start(f32[64,512]{1,0:T(8,128)S(1)} %slice_select_fusion), channel_id=1, source_target_pairs={{0,4},{2,6},{4,0},{6,2},{8,12},{10,14},{12,8},{14,10},{16,20},{18,... | collective-permute-start | bytes 393224 | tf_op jit(solution)/shard_map/ppermute | solution.py:310
  61.9 5.1 %collective-permute-start.9 = (f32[64,512]{1,0:T(8,128)S(1)}, f32[64,512]{1,0:T(8,128)S(1)}, u32[]{:S(2)}, u32[]{:S(2)}) collective-permute-start(f32[64,512]{1,0:T(8,128)S(1)} %select_select_fusion), channel_id=1, source_target_pairs={{0,8},{2,10},{4,12},{6,14},{8,0},{10,2},{12,4},{14,6},{16,24},{18,... | collective-permute-start | bytes 393224 | tf_op jit(solution)/shard_map/ppermute | solution.py:310
  67.0 8.5 %collective-permute-start.10 = (f32[64,512]{1,0:T(8,128)S(1)}, f32[64,512]{1,0:T(8,128)S(1)}, u32[]{:S(2)}, u32[]{:S(2)}) collective-permute-start(f32[64,512]{1,0:T(8,128)S(1)} %broadcast_select_fusion.2), channel_id=1, source_target_pairs={{0,16},{2,18},{4,20},{6,22},{8,24},{10,26},{12,28},{14,30},{16,0},... | collective-permute-start | bytes 393224 | tf_op jit(solution)/shard_map/ppermute | solution.py:310
  75.5 8.7 %copy-start.3 = (f32[64,512]{1,0:T(8,128)}, f32[64,512]{1,0:T(8,128)S(1)}, u32[]{:S(2)}) copy-start(f32[64,512]{1,0:T(8,128)S(1)} %broadcast_select_fusion.3.refs_0_) | copy-start | bytes 393220
  75.5 5.8 %collective-permute-start.13 = (f32[64,512]{1,0:T(8,128)S(1)}, f32[64,512]{1,0:T(8,128)S(1)}, u32[]{:S(2)}, u32[]{:S(2)}) collective-permute-start(f32[64,512]{1,0:T(8,128)S(1)} %broadcast_select_fusion.3.refs_0_), channel_id=1, source_target_pairs={{0,6},{2,4},{4,2},{6,0},{8,14},{10,12},{12,10},{14,8},{16,22},{18,... | collective-permute-start | bytes 393224 | tf_op jit(solution)/shard_map/ppermute | solution.py:310
  75.8 5.6 %collective-permute-start.12 = (f32[64,512]{1,0:T(8,128)S(1)}, f32[64,512]{1,0:T(8,128)S(1)}, u32[]{:S(2)}, u32[]{:S(2)}) collective-permute-start(f32[64,512]{1,0:T(8,128)S(1)} %broadcast_select_fusion.3.refs_0_), channel_id=1, source_target_pairs={{0,2},{2,0},{4,6},{6,4},{8,10},{10,8},{12,14},{14,12},{16,18},{18,... | collective-permute-start | bytes 393224 | tf_op jit(solution)/shard_map/ppermute | solution.py:310
  77.2 7.0 %collective-permute-start.11 = (f32[64,512]{1,0:T(8,128)S(1)}, f32[64,512]{1,0:T(8,128)S(1)}, u32[]{:S(2)}, u32[]{:S(2)}) collective-permute-start(f32[64,512]{1,0:T(8,128)S(1)} %broadcast_select_fusion.3.refs_0_), channel_id=1, source_target_pairs={{0,4},{2,6},{4,0},{6,2},{8,12},{10,14},{12,8},{14,10},{16,20},{18,... | collective-permute-start | bytes 393224 | tf_op jit(solution)/shard_map/ppermute | solution.py:310
  81.3 2.8 %copy-start.5 = (f32[64,512]{1,0:T(8,128)}, f32[64,512]{1,0:T(8,128)S(1)}, u32[]{:S(2)}) copy-start(f32[64,512]{1,0:T(8,128)S(1)} %collective-permute-done.13.refs_3_) | copy-start | bytes 393220
  81.3 2.8 %copy-start.6 = (f32[64,512]{1,0:T(8,128)}, f32[64,512]{1,0:T(8,128)S(1)}, u32[]{:S(2)}) copy-start(f32[64,512]{1,0:T(8,128)S(1)} %collective-permute-done.12.refs_2_) | copy-start | bytes 393220
  84.2 0.7 copy-start.7
  90.4 2.2 %copy-start = (f32[4096,2,128]{2,1,0:T(2,128)S(1)}, f32[4096,2,128]{2,1,0:T(2,128)}, u32[]{:S(2)}) copy-start(f32[4096,2,128]{2,1,0:T(2,128)} %param.16) | copy-start | bytes 12582916
  92.6 1.1 %copy-start.2 = (bf16[768,512]{1,0:T(8,128)(2,1)S(1)}, bf16[768,512]{1,0:T(8,128)(2,1)}, u32[]{:S(2)}) copy-start(bf16[768,512]{1,0:T(8,128)(2,1)} %get-tuple-element.20.terms_ref) | copy-start | bytes 2359300
  93.7 8.1 %copy-start.1 = (bf16[768,512]{1,0:T(8,128)(2,1)S(1)}, bf16[768,512]{1,0:T(8,128)(2,1)}, u32[]{:S(2)}) copy-start(bf16[768,512]{1,0:T(8,128)(2,1)} %get-tuple-element.21.terms_ref) | copy-start | bytes 2359300

commit v3 on v0

--- a/solution.py
+++ b/solution.py
@@ -10,7 +10,7 @@
 
 SUB = 32
 GROUP = 8
-VMEM_BYTES = 57 * 1024 * 1024
+VMEM_BYTES = 48 * 1024 * 1024
 ADD_VMEM_BYTES = 48 * 1024 * 1024
 FULL_VMEM_BYTES = 59 * 1024 * 1024
 TILE = 512

time: 109 us -> 108 us (level)
  waiting for transfers between devices: 47.5 us -> 43.2 us
  other arithmetic: 0.92 us -> 4.2 us
  Pallas kernels: 34.8 us -> 33.2 us
    ppermute x1, waiting for transfers between devices: 6.38 us -> 2.29 us  [on_device(): lax.ppermute(own, 'col', [(i, (i + step) % col_size) for i in range(col_s...]
    select_n x2, other arithmetic: 0.09 us -> 2.14 us  [spread(): kept = jnp.where(apart == 0, kept, exchange(given, 1))]
    select_n x2, other arithmetic: 0.05 us -> 1.88 us  [spread(): kept = jnp.where(apart < 2, kept, exchange(given, 2))]
    pallas_call x1, Pallas kernels: 5.61 us -> 4.08 us  [finish_sides(): pl.pallas_call(finish_kernel, out_shape=(jax.ShapeDtypeStruct(sides.shape...]
    unnamed x20 -> x28, local copies, waits for them, and re-layouts: 2.71 us -> 3.12 us
  transfers between devices with their start and end apart: 15 -> 15, of which waited for: 11 -> 11; matrix products, arithmetic and copies ran while one was open for 2% -> 5% of each run, Pallas kernels for 20% -> 19%
where the time goes in v3:
time: 108 us; the launch traced here: 107 us
  waiting for transfers between devices  43.2 us (40%)
  Pallas kernels  33.2 us (31%)
  starting transfers between devices  17.4 us (16%)
  between operations  4.81 us (4%)
  local copies, waits for them, and re-layouts  4.51 us (4%)
  other arithmetic  4.2 us (4%)
    ppermute x14, waiting for transfers between devices, exchange(): return lax.ppermute(value, axis, [(i, i ^ bit) for i in range(size)])  40.9 us
    ppermute x14, starting transfers between devices, exchange(): return lax.ppermute(value, axis, [(i, i ^ bit) for i in range(size)])  14.4 us
    pallas_call x1, Pallas kernels, add_product(): pl.pallas_call(functools.partial(add_kernel, paired), out_shape=jax.Shape...  12.8 us
    pallas_call x1, Pallas kernels, solve_upper(): pl.pallas_call(upper_kernel, out_shape=(*[jax.ShapeDtypeStruct((block //...  8.61 us
    pallas_call x1, Pallas kernels, solve_lower(): pl.pallas_call(lower_kernel, out_shape=(*[jax.ShapeDtypeStruct((block //...  7.7 us
    pallas_call x1, Pallas kernels, finish_sides(): pl.pallas_call(finish_kernel, out_shape=(jax.ShapeDtypeStruct(sides.shape...  4.08 us
    unnamed x28, local copies, waits for them, and re-layouts  3.12 us
    ppermute x1, starting transfers between devices, on_device(): lax.ppermute(own, 'col', [(i, (i + step) % col_size) for i in range(col_s...  3.03 us
  transfers between devices with their start and end apart: 15, of which 11 were waited for; matrix products, arithmetic and copies ran while one was open for 5% of the time, Pallas kernels for 19%

profile of v3, /device:TPU:0, one launch (start us, length us, event | category | flops | bytes accessed | tf_op | source)
XLA Modules:
  0.0 107.4 jit_solution(16899898875923080462)
XLA Ops:
  0.6 3.0 %collective-permute-start.14 = (f32[8192,128]{1,0:T(8,128)}, f32[8192,128]{1,0:T(8,128)}, u32[]{:S(2)}, u32[]{:S(2)}) collective-permute-start(f32[8192,128]{1,0:T(8,128)} %bitcast.9), channel_id=1, source_target_pairs={{0,1},{1,0},{2,3},{3,2},{4,5},{5,4},{6,7},{7,6},{8,9},{9,8},{10,11... | collective-permute-start | bytes 12582920 | tf_op jit(solution)/shard_map/ppermute | solution.py:349
  3.7 7.7 %solve_lower.1 = (f32[128,512]{1,0:T(8,128)}, f32[128,512]{1,0:T(8,128)}, f32[1,512]{1,0:T(1,128)}, f32[1,512]{1,0:T(1,128)}) custom-call(s32[32]{0:T(128)} %slots.5, s32[1]{0:T(128)} %bitcast.me, f32[512,512]{1,0:T(8,128)} %s_ref.5, f32[512,512]{1,0:T(8,128)} %t_ref.5, f32[512,512]{1,0:T(8,128)} %r_ref.5, f32[32,128]{1,0:T(8,128)} %bitcast.11, ...), custom_call_target="tpu_custom_call" | custom-call | flops 1000 | bytes 1000 | tf_op jit(solution)/shard_map/solve_lower/pallas_call | solution.py:146
  11.4 0.0 collective-permute-start
  11.4 1.4 %fusion = (s32[1]{0:T(128)}, s32[1]{0:T(128)}) fusion(s32[32]{0:T(128)} %slots.5), kind=kLoop, calls=%fused_computation.11 | loop fusion | bytes 16 | tf_op jit(solution)/shard_map/slice | solution.py:343
  14.7 0.0 collective-permute-done
  14.7 0.0 copy-start.9
  14.7 0.7 copy-done.9
  15.4 0.0 copy-start
  15.4 0.0 copy-start.1
  15.4 0.0 copy-start.2
  15.4 0.0 copy-start.5
  15.4 0.0 copy-start.6
  15.4 0.0 copy-start.7
  15.4 1.1 %broadcast_select_fusion.1 = f32[128,512]{1,0:T(8,128)S(1)} fusion(f32[128,512]{1,0:T(8,128)} %get-tuple-element.13, f32[128,512]{1,0:T(8,128)} %copy-done.9, pred[]{:T(512)S(6)} %eq.13), kind=kLoop, calls=%fused_computation.3 | loop fusion | flops 65536 | bytes 786433 | tf_op jit(solution)/shard_map/jit(_where)/select_n | solution.py:312
  16.6 1.6 %collective-permute-start.1 = (f32[64,512]{1,0:T(8,128)S(1)}, f32[64,512]{1,0:T(8,128)}, u32[]{:S(2)}, u32[]{:S(2)}) collective-permute-start(f32[64,512]{1,0:T(8,128)S(1)} %slice_select_fusion.1), channel_id=1, source_target_pairs={{0,4},{2,6},{4,0},{6,2},{8,12},{10,14},{12,8},{14,10},{16,20},{18,... | collective-permute-start | bytes 393224 | tf_op jit(solution)/shard_map/ppermute | solution.py:309
  18.2 4.5 %collective-permute-done.1 = f32[64,512]{1,0:T(8,128)} collective-permute-done((f32[64,512]{1,0:T(8,128)S(1)}, f32[64,512]{1,0:T(8,128)}, u32[]{:S(2)}, u32[]{:S(2)}) %collective-permute-start.1) | collective-permute-done | bytes 131104 | tf_op jit(solution)/shard_map/ppermute | solution.py:309
  22.7 0.9 select_select_fusion.1
  23.6 1.6 %collective-permute-start.2 = (f32[64,512]{1,0:T(8,128)S(1)}, f32[64,512]{1,0:T(8,128)S(1)}, u32[]{:S(2)}, u32[]{:S(2)}) collective-permute-start(f32[64,512]{1,0:T(8,128)S(1)} %select_select_fusion.1), channel_id=1, source_target_pairs={{0,8},{2,10},{4,12},{6,14},{8,0},{10,2},{12,4},{14,6},{16,24},{18,... | collective-permute-start | bytes 393224 | tf_op jit(solution)/shard_map/ppermute | solution.py:309
  25.3 3.6 %collective-permute-done.2 = f32[64,512]{1,0:T(8,128)S(1)} collective-permute-done((f32[64,512]{1,0:T(8,128)S(1)}, f32[64,512]{1,0:T(8,128)S(1)}, u32[]{:S(2)}, u32[]{:S(2)}) %collective-permute-start.2) | collective-permute-done | bytes 131104 | tf_op jit(solution)/shard_map/ppermute | solution.py:309
  28.8 2.6 %collective-permute-start.3 = (f32[64,512]{1,0:T(8,128)S(1)}, f32[64,512]{1,0:T(8,128)S(1)}, u32[]{:S(2)}, u32[]{:S(2)}) collective-permute-start(f32[64,512]{1,0:T(8,128)S(1)} %broadcast_select_fusion.4), channel_id=1, source_target_pairs={{0,16},{2,18},{4,20},{6,22},{8,24},{10,26},{12,28},{14,30},{16,0},... | collective-permute-start | bytes 393224 | tf_op jit(solution)/shard_map/ppermute | solution.py:309
  31.5 5.5 %collective-permute-done.3 = f32[64,512]{1,0:T(8,128)S(1)} collective-permute-done((f32[64,512]{1,0:T(8,128)S(1)}, f32[64,512]{1,0:T(8,128)S(1)}, u32[]{:S(2)}, u32[]{:S(2)}) %collective-permute-start.3) | collective-permute-done | bytes 131104 | tf_op jit(solution)/shard_map/ppermute | solution.py:309
  37.0 0.0 copy-start.8
  37.0 0.4 collective-permute-start.6
  37.4 1.4 %collective-permute-start.5 = (f32[64,512]{1,0:T(8,128)S(1)}, f32[64,512]{1,0:T(8,128)S(1)}, u32[]{:S(2)}, u32[]{:S(2)}) collective-permute-start(f32[64,512]{1,0:T(8,128)S(1)} %broadcast_select_fusion.5.refs_0_), channel_id=1, source_target_pairs={{0,2},{2,0},{4,6},{6,4},{8,10},{10,8},{12,14},{14,12},{16,18},{18,... | collective-permute-start | bytes 393224 | tf_op jit(solution)/shard_map/ppermute | solution.py:309
  38.8 0.4 collective-permute-start.4
  39.2 3.5 %collective-permute-done.6.refs_3_ = f32[64,512]{1,0:T(8,128)S(1)} collective-permute-done((f32[64,512]{1,0:T(8,128)S(1)}, f32[64,512]{1,0:T(8,128)S(1)}, u32[]{:S(2)}, u32[]{:S(2)}) %collective-permute-start.6) | collective-permute-done | bytes 131104 | tf_op jit(solution)/shard_map/ppermute | solution.py:309
  42.7 0.0 collective-permute-done.5.refs_2_
  42.7 3.0 %collective-permute-done.4.refs_1_ = f32[64,512]{1,0:T(8,128)S(1)} collective-permute-done((f32[64,512]{1,0:T(8,128)S(1)}, f32[64,512]{1,0:T(8,128)S(1)}, u32[]{:S(2)}, u32[]{:S(2)}) %collective-permute-start.4) | collective-permute-done | bytes 131104 | tf_op jit(solution)/shard_map/ppermute | solution.py:309
  45.7 0.0 copy-done.8
  45.7 0.0 copy-done.11
  45.7 0.0 copy-done.12
  45.7 0.6 copy-done.13
  46.3 8.6 %solve_upper.1 = (f32[128,512]{1,0:T(8,128)}, f32[128,512]{1,0:T(8,128)}, f32[256,512]{1,0:T(8,128)}) custom-call(s32[32]{0:T(128)} %slots.5, s32[1]{0:T(128)} %bitcast.me, f32[512,512]{1,0:T(8,128)} %s_ref.5, f32[512,512]{1,0:T(8,128)} %t_ref.5, f32[512,512]{1,0:T(8,128)} %r_ref.5, f32[1,512]{1,0:T(1,128)} %get-tuple-element.11.alpha_ref, ...), custom_call_target="tpu_custom_call" | custom-call | flops 1000 | bytes 1000 | tf_op jit(solution)/shard_map/solve_upper/pallas_call | solution.py:182
  54.9 0.0 collective-permute-start.7
  57.0 0.0 collective-permute-done.7
  57.0 0.0 copy-start.10
  57.1 0.7 copy-done.10
  57.8 1.0 broadcast_select_fusion
  58.8 1.2 %collective-permute-start.8 = (f32[64,512]{1,0:T(8,128)S(1)}, f32[64,512]{1,0:T(8,128)}, u32[]{:S(2)}, u32[]{:S(2)}) collective-permute-start(f32[64,512]{1,0:T(8,128)S(1)} %slice_select_fusion), channel_id=1, source_target_pairs={{0,4},{2,6},{4,0},{6,2},{8,12},{10,14},{12,8},{14,10},{16,20},{18,... | collective-permute-start | bytes 393224 | tf_op jit(solution)/shard_map/ppermute | solution.py:309
  60.0 4.9 %collective-permute-done.8 = f32[64,512]{1,0:T(8,128)} collective-permute-done((f32[64,512]{1,0:T(8,128)S(1)}, f32[64,512]{1,0:T(8,128)}, u32[]{:S(2)}, u32[]{:S(2)}) %collective-permute-start.8) | collective-permute-done | bytes 131104 | tf_op jit(solution)/shard_map/ppermute | solution.py:309
  64.8 0.9 select_select_fusion
  65.8 0.7 collective-permute-start.9
  66.5 4.4 %collective-permute-done.9 = f32[64,512]{1,0:T(8,128)S(1)} collective-permute-done((f32[64,512]{1,0:T(8,128)S(1)}, f32[64,512]{1,0:T(8,128)S(1)}, u32[]{:S(2)}, u32[]{:S(2)}) %collective-permute-start.9) | collective-permute-done | bytes 131104 | tf_op jit(solution)/shard_map/ppermute | solution.py:309
  71.0 2.2 %collective-permute-start.10 = (f32[64,512]{1,0:T(8,128)S(1)}, f32[64,512]{1,0:T(8,128)S(1)}, u32[]{:S(2)}, u32[]{:S(2)}) collective-permute-start(f32[64,512]{1,0:T(8,128)S(1)} %broadcast_select_fusion.2), channel_id=1, source_target_pairs={{0,16},{2,18},{4,20},{6,22},{8,24},{10,26},{12,28},{14,30},{16,0},... | collective-permute-start | bytes 393224 | tf_op jit(solution)/shard_map/ppermute | solution.py:309
  73.2 5.9 %collective-permute-done.10 = f32[64,512]{1,0:T(8,128)S(1)} collective-permute-done((f32[64,512]{1,0:T(8,128)S(1)}, f32[64,512]{1,0:T(8,128)S(1)}, u32[]{:S(2)}, u32[]{:S(2)}) %collective-permute-start.10) | collective-permute-done | bytes 131104 | tf_op jit(solution)/shard_map/ppermute | solution.py:309
  79.1 0.1 collective-permute-start.13
  79.2 0.1 collective-permute-start.12
  79.3 2.0 %collective-permute-start.11 = (f32[64,512]{1,0:T(8,128)S(1)}, f32[64,512]{1,0:T(8,128)}, u32[]{:S(2)}, u32[]{:S(2)}) collective-permute-start(f32[64,512]{1,0:T(8,128)S(1)} %broadcast_select_fusion.3.refs_0_), channel_id=1, source_target_pairs={{0,4},{2,6},{4,0},{6,2},{8,12},{10,14},{12,8},{14,10},{16,20},{18,... | collective-permute-start | bytes 393224 | tf_op jit(solution)/shard_map/ppermute | solution.py:309
  81.3 0.1 pad_add_fusion.parts
  81.4 3.5 %collective-permute-done.13.refs_3_ = f32[64,512]{1,0:T(8,128)S(1)} collective-permute-done((f32[64,512]{1,0:T(8,128)S(1)}, f32[64,512]{1,0:T(8,128)S(1)}, u32[]{:S(2)}, u32[]{:S(2)}) %collective-permute-start.13) | collective-permute-done | bytes 131104 | tf_op jit(solution)/shard_map/ppermute | solution.py:309
  84.9 0.0 collective-permute-done.12.refs_2_
  84.9 2.2 %collective-permute-done.11.refs_1_ = f32[64,512]{1,0:T(8,128)} collective-permute-done((f32[64,512]{1,0:T(8,128)S(1)}, f32[64,512]{1,0:T(8,128)}, u32[]{:S(2)}, u32[]{:S(2)}) %collective-permute-start.11) | collective-permute-done | bytes 131104 | tf_op jit(solution)/shard_map/ppermute | solution.py:309
  87.1 0.0 copy-done
  87.1 0.0 copy-done.1
  87.1 0.0 copy-done.2
  87.1 0.0 copy-done.5
  87.1 0.0 copy-done.6
  87.1 0.0 copy-done.7
  87.1 0.0 copy-start.4
  87.2 1.0 copy-done.4
  88.2 4.1 %finish_sides.1 = (f32[512,512]{1,0:T(8,128)}, bf16[1536,512]{1,0:T(8,128)(2,1)S(1)}) custom-call(s32[32]{0:T(128)S(1)} %copy-done.5, s32[1]{0:T(128)} %bitcast.me, s32[2]{0:T(128)S(1)} %pad_add_fusion.parts, f32[512,512]{1,0:T(8,128)S(1)} %copy-done, f32[512,512]{1,0:T(8,128)S(1)} %copy-done.1, f32[512,512]{1,0:T(8,128)S(1)} %copy-done.2, ...), custom_call_target="tpu_custom_call" | custom-call | flops 1000 | bytes 1000 | tf_op jit(solution)/shard_map/finish_sides/pallas_call | solution.py:245
  92.3 2.3 %collective-permute-done.14.refs_1_ = f32[8192,128]{1,0:T(8,128)} collective-permute-done((f32[8192,128]{1,0:T(8,128)}, f32[8192,128]{1,0:T(8,128)}, u32[]{:S(2)}, u32[]{:S(2)}) %collective-permute-start.14) | collective-permute-done | bytes 4194336 | tf_op jit(solution)/shard_map/ppermute | solution.py:349
  94.6 0.0 copy-done.3
  94.6 12.8 %add_product.1 = f32[4096,512]{1,0:T(8,128)} custom-call(f32[4096,512]{1,0:T(8,128)} %base_ref.1, bf16[1536,512]{1,0:T(8,128)(2,1)S(1)} %get-tuple-element.19.terms_ref, f32[8192,128]{1,0:T(8,128)S(1)} %bitcast.10, f32[8192,128]{1,0:T(8,128)} %collective-permute-done.14.refs_1_), custom_call_target="tpu_custom_call" | custom-call | flops 1000 | bytes 1000 | tf_op jit(solution)/shard_map/add_product/pallas_call | solution.py:282
  (10 shorter events, 0.1 us)
Async XLA Ops:
  0.6 93.9 %collective-permute-start.14 = (f32[8192,128]{1,0:T(8,128)}, f32[8192,128]{1,0:T(8,128)}, u32[]{:S(2)}, u32[]{:S(2)}) collective-permute-start(f32[8192,128]{1,0:T(8,128)} %bitcast.9), channel_id=1, source_target_pairs={{0,1},{1,0},{2,3},{3,2},{4,5},{5,4},{6,7},{7,6},{8,9},{9,8},{10,11... | collective-permute-start | bytes 12582920 | tf_op jit(solution)/shard_map/ppermute | solution.py:349
  11.4 3.3 %collective-permute-start = (f32[128,512]{1,0:T(8,128)}, f32[128,512]{1,0:T(8,128)S(1)}, u32[]{:S(2)}, u32[]{:S(2)}) collective-permute-start(f32[128,512]{1,0:T(8,128)} %get-tuple-element.14), channel_id=1, source_target_pairs={{0,2},{2,0},{4,6},{6,4},{8,10},{10,8},{12,14},{14,12},{16,18},{18,... | collective-permute-start | bytes 786440 | tf_op jit(solution)/shard_map/ppermute | solution.py:309
  14.7 0.7 copy-start.9
  15.4 71.7 %copy-start = (f32[512,512]{1,0:T(8,128)S(1)}, f32[512,512]{1,0:T(8,128)}, u32[]{:S(2)}) copy-start(f32[512,512]{1,0:T(8,128)} %r_ref.5) | copy-start | bytes 3145732
  15.4 71.7 %copy-start.1 = (f32[512,512]{1,0:T(8,128)S(1)}, f32[512,512]{1,0:T(8,128)}, u32[]{:S(2)}) copy-start(f32[512,512]{1,0:T(8,128)} %s_ref.5) | copy-start | bytes 3145732
  15.4 71.7 %copy-start.2 = (f32[512,512]{1,0:T(8,128)S(1)}, f32[512,512]{1,0:T(8,128)}, u32[]{:S(2)}) copy-start(f32[512,512]{1,0:T(8,128)} %t_ref.5) | copy-start | bytes 3145732
  15.4 71.7 %copy-start.5 = (s32[32]{0:T(128)S(1)}, s32[32]{0:T(128)}, u32[]{:S(2)}) copy-start(s32[32]{0:T(128)} %slots.5) | copy-start | bytes 388
  15.4 71.7 %copy-start.6 = (f32[1,512]{1,0:T(1,128)S(1)}, f32[1,512]{1,0:T(1,128)}, u32[]{:S(2)}) copy-start(f32[1,512]{1,0:T(1,128)} %get-tuple-element.11.alpha_ref) | copy-start | bytes 6148
  15.4 71.7 %copy-start.7 = (f32[1,512]{1,0:T(1,128)S(1)}, f32[1,512]{1,0:T(1,128)}, u32[]{:S(2)}) copy-start(f32[1,512]{1,0:T(1,128)} %get-tuple-element.12.beta_ref) | copy-start | bytes 6148
  16.6 6.1 %collective-permute-start.1 = (f32[64,512]{1,0:T(8,128)S(1)}, f32[64,512]{1,0:T(8,128)}, u32[]{:S(2)}, u32[]{:S(2)}) collective-permute-start(f32[64,512]{1,0:T(8,128)S(1)} %slice_select_fusion.1), channel_id=1, source_target_pairs={{0,4},{2,6},{4,0},{6,2},{8,12},{10,14},{12,8},{14,10},{16,20},{18,... | collective-permute-start | bytes 393224 | tf_op jit(solution)/shard_map/ppermute | solution.py:309
  23.6 5.2 %collective-permute-start.2 = (f32[64,512]{1,0:T(8,128)S(1)}, f32[64,512]{1,0:T(8,128)S(1)}, u32[]{:S(2)}, u32[]{:S(2)}) collective-permute-start(f32[64,512]{1,0:T(8,128)S(1)} %select_select_fusion.1), channel_id=1, source_target_pairs={{0,8},{2,10},{4,12},{6,14},{8,0},{10,2},{12,4},{14,6},{16,24},{18,... | collective-permute-start | bytes 393224 | tf_op jit(solution)/shard_map/ppermute | solution.py:309
  28.8 8.1 %collective-permute-start.3 = (f32[64,512]{1,0:T(8,128)S(1)}, f32[64,512]{1,0:T(8,128)S(1)}, u32[]{:S(2)}, u32[]{:S(2)}) collective-permute-start(f32[64,512]{1,0:T(8,128)S(1)} %broadcast_select_fusion.4), channel_id=1, source_target_pairs={{0,16},{2,18},{4,20},{6,22},{8,24},{10,26},{12,28},{14,30},{16,0},... | collective-permute-start | bytes 393224 | tf_op jit(solution)/shard_map/ppermute | solution.py:309
  37.0 8.7 %copy-start.8 = (f32[64,512]{1,0:T(8,128)}, f32[64,512]{1,0:T(8,128)S(1)}, u32[]{:S(2)}) copy-start(f32[64,512]{1,0:T(8,128)S(1)} %broadcast_select_fusion.5.refs_0_) | copy-start | bytes 393220
  37.0 5.7 %collective-permute-start.6 = (f32[64,512]{1,0:T(8,128)S(1)}, f32[64,512]{1,0:T(8,128)S(1)}, u32[]{:S(2)}, u32[]{:S(2)}) collective-permute-start(f32[64,512]{1,0:T(8,128)S(1)} %broadcast_select_fusion.5.refs_0_), channel_id=1, source_target_pairs={{0,6},{2,4},{4,2},{6,0},{8,14},{10,12},{12,10},{14,8},{16,22},{18,... | collective-permute-start | bytes 393224 | tf_op jit(solution)/shard_map/ppermute | solution.py:309
  37.4 5.3 %collective-permute-start.5 = (f32[64,512]{1,0:T(8,128)S(1)}, f32[64,512]{1,0:T(8,128)S(1)}, u32[]{:S(2)}, u32[]{:S(2)}) collective-permute-start(f32[64,512]{1,0:T(8,128)S(1)} %broadcast_select_fusion.5.refs_0_), channel_id=1, source_target_pairs={{0,2},{2,0},{4,6},{6,4},{8,10},{10,8},{12,14},{14,12},{16,18},{18,... | collective-permute-start | bytes 393224 | tf_op jit(solution)/shard_map/ppermute | solution.py:309
  38.8 6.8 %collective-permute-start.4 = (f32[64,512]{1,0:T(8,128)S(1)}, f32[64,512]{1,0:T(8,128)S(1)}, u32[]{:S(2)}, u32[]{:S(2)}) collective-permute-start(f32[64,512]{1,0:T(8,128)S(1)} %broadcast_select_fusion.5.refs_0_), channel_id=1, source_target_pairs={{0,4},{2,6},{4,0},{6,2},{8,12},{10,14},{12,8},{14,10},{16,20},{18,... | collective-permute-start | bytes 393224 | tf_op jit(solution)/shard_map/ppermute | solution.py:309
  42.7 3.0 %copy-start.11 = (f32[64,512]{1,0:T(8,128)}, f32[64,512]{1,0:T(8,128)S(1)}, u32[]{:S(2)}) copy-start(f32[64,512]{1,0:T(8,128)S(1)} %collective-permute-done.6.refs_3_) | copy-start | bytes 393220
  42.7 3.0 %copy-start.12 = (f32[64,512]{1,0:T(8,128)}, f32[64,512]{1,0:T(8,128)S(1)}, u32[]{:S(2)}) copy-start(f32[64,512]{1,0:T(8,128)S(1)} %collective-permute-done.5.refs_2_) | copy-start | bytes 393220
  45.7 0.7 copy-start.13
  54.9 2.1 %collective-permute-start.7 = (f32[128,512]{1,0:T(8,128)}, f32[128,512]{1,0:T(8,128)S(1)}, u32[]{:S(2)}, u32[]{:S(2)}) collective-permute-start(f32[128,512]{1,0:T(8,128)} %get-tuple-element.17), channel_id=1, source_target_pairs={{0,2},{2,0},{4,6},{6,4},{8,10},{10,8},{12,14},{14,12},{16,18},{18,... | collective-permute-start | bytes 786440 | tf_op jit(solution)/shard_map/ppermute | solution.py:309
  57.0 0.7 copy-start.10
  58.8 6.1 %collective-permute-start.8 = (f32[64,512]{1,0:T(8,128)S(1)}, f32[64,512]{1,0:T(8,128)}, u32[]{:S(2)}, u32[]{:S(2)}) collective-permute-start(f32[64,512]{1,0:T(8,128)S(1)} %slice_select_fusion), channel_id=1, source_target_pairs={{0,4},{2,6},{4,0},{6,2},{8,12},{10,14},{12,8},{14,10},{16,20},{18,... | collective-permute-start | bytes 393224 | tf_op jit(solution)/shard_map/ppermute | solution.py:309
  65.8 5.2 %collective-permute-start.9 = (f32[64,512]{1,0:T(8,128)S(1)}, f32[64,512]{1,0:T(8,128)S(1)}, u32[]{:S(2)}, u32[]{:S(2)}) collective-permute-start(f32[64,512]{1,0:T(8,128)S(1)} %select_select_fusion), channel_id=1, source_target_pairs={{0,8},{2,10},{4,12},{6,14},{8,0},{10,2},{12,4},{14,6},{16,24},{18,... | collective-permute-start | bytes 393224 | tf_op jit(solution)/shard_map/ppermute | solution.py:309
  71.0 8.1 %collective-permute-start.10 = (f32[64,512]{1,0:T(8,128)S(1)}, f32[64,512]{1,0:T(8,128)S(1)}, u32[]{:S(2)}, u32[]{:S(2)}) collective-permute-start(f32[64,512]{1,0:T(8,128)S(1)} %broadcast_select_fusion.2), channel_id=1, source_target_pairs={{0,16},{2,18},{4,20},{6,22},{8,24},{10,26},{12,28},{14,30},{16,0},... | collective-permute-start | bytes 393224 | tf_op jit(solution)/shard_map/ppermute | solution.py:309
  79.1 5.8 %collective-permute-start.13 = (f32[64,512]{1,0:T(8,128)S(1)}, f32[64,512]{1,0:T(8,128)S(1)}, u32[]{:S(2)}, u32[]{:S(2)}) collective-permute-start(f32[64,512]{1,0:T(8,128)S(1)} %broadcast_select_fusion.3.refs_0_), channel_id=1, source_target_pairs={{0,6},{2,4},{4,2},{6,0},{8,14},{10,12},{12,10},{14,8},{16,22},{18,... | collective-permute-start | bytes 393224 | tf_op jit(solution)/shard_map/ppermute | solution.py:309
  79.2 5.7 %collective-permute-start.12 = (f32[64,512]{1,0:T(8,128)S(1)}, f32[64,512]{1,0:T(8,128)S(1)}, u32[]{:S(2)}, u32[]{:S(2)}) collective-permute-start(f32[64,512]{1,0:T(8,128)S(1)} %broadcast_select_fusion.3.refs_0_), channel_id=1, source_target_pairs={{0,2},{2,0},{4,6},{6,4},{8,10},{10,8},{12,14},{14,12},{16,18},{18,... | collective-permute-start | bytes 393224 | tf_op jit(solution)/shard_map/ppermute | solution.py:309
  79.3 7.8 %collective-permute-start.11 = (f32[64,512]{1,0:T(8,128)S(1)}, f32[64,512]{1,0:T(8,128)}, u32[]{:S(2)}, u32[]{:S(2)}) collective-permute-start(f32[64,512]{1,0:T(8,128)S(1)} %broadcast_select_fusion.3.refs_0_), channel_id=1, source_target_pairs={{0,4},{2,6},{4,0},{6,2},{8,12},{10,14},{12,8},{14,10},{16,20},{18,... | collective-permute-start | bytes 393224 | tf_op jit(solution)/shard_map/ppermute | solution.py:309
  81.3 13.2 %copy-start.3 = (f32[4096,2,128]{2,1,0:T(2,128)S(1)}, f32[4096,2,128]{2,1,0:T(2,128)}, u32[]{:S(2)}) copy-start(f32[4096,2,128]{2,1,0:T(2,128)} %param.16) | copy-start | bytes 12582916
  87.1 1.0 copy-start.4

commit v4 on v3

--- a/solution.py
+++ b/solution.py
@@ -13,7 +13,7 @@
 VMEM_BYTES = 48 * 1024 * 1024
 ADD_VMEM_BYTES = 48 * 1024 * 1024
 FULL_VMEM_BYTES = 59 * 1024 * 1024
-TILE = 512
+TILE = 1024
 LIGHT = pl.CostEstimate(flops=1000, bytes_accessed=1000, transcendentals=0)
 
 

time: 108 us -> 106 us (0.981)
  starting transfers between devices: 17.4 us -> 15.5 us
  waiting for transfers between devices: 43.2 us -> 44.9 us
  Pallas kernels: 33.2 us -> 32 us
    ppermute x14, starting transfers between devices: 14.4 us -> 12.5 us  [exchange(): return lax.ppermute(value, axis, [(i, i ^ bit) for i in range(size)])]
    pallas_call x1, Pallas kernels: 12.8 us -> 11.4 us  [add_product(): pl.pallas_call(functools.partial(add_kernel, paired), out_shape=jax.Shape...]
    ppermute x14, waiting for transfers between devices: 40.9 us -> 42.3 us  [exchange(): return lax.ppermute(value, axis, [(i, i ^ bit) for i in range(size)])]
where the time goes in v4:
time: 106 us
  waiting for transfers between devices  44.9 us (42%)
  Pallas kernels  32 us (30%)
  starting transfers between devices  15.5 us (15%)
  between operations  4.83 us (5%)
  local copies, waits for them, and re-layouts  4.51 us (4%)
  other arithmetic  4.2 us (4%)
    ppermute x14, waiting for transfers between devices, exchange(): return lax.ppermute(value, axis, [(i, i ^ bit) for i in range(size)])  42.3 us
    ppermute x14, starting transfers between devices, exchange(): return lax.ppermute(value, axis, [(i, i ^ bit) for i in range(size)])  12.5 us
    pallas_call x1, Pallas kernels, add_product(): pl.pallas_call(functools.partial(add_kernel, paired), out_shape=jax.Shape...  11.4 us
    pallas_call x1, Pallas kernels, solve_upper(): pl.pallas_call(upper_kernel, out_shape=(*[jax.ShapeDtypeStruct((block //...  8.61 us
    pallas_call x1, Pallas kernels, solve_lower(): pl.pallas_call(lower_kernel, out_shape=(*[jax.ShapeDtypeStruct((block //...  7.7 us
    pallas_call x1, Pallas kernels, finish_sides(): pl.pallas_call(finish_kernel, out_shape=(jax.ShapeDtypeStruct(sides.shape...  4.27 us
    unnamed x28, local copies, waits for them, and re-layouts  3.12 us
    ppermute x1, starting transfers between devices, on_device(): lax.ppermute(own, 'col', [(i, (i + step) % col_size) for i in range(col_s...  3.03 us
  transfers between devices with their start and end apart: 15, of which 11 were waited for; matrix products, arithmetic and copies ran while one was open for 5% of the time, Pallas kernels for 19%

profile of v4, /device:TPU:0, one launch (start us, length us, event | category | flops | bytes accessed | tf_op | source)
XLA Modules:
  0.0 105.9 jit_solution(8335718128033015844)
XLA Ops:
  0.6 3.0 %collective-permute-start.14 = (f32[8192,128]{1,0:T(8,128)}, f32[8192,128]{1,0:T(8,128)}, u32[]{:S(2)}, u32[]{:S(2)}) collective-permute-start(f32[8192,128]{1,0:T(8,128)} %bitcast.9), channel_id=1, source_target_pairs={{0,1},{1,0},{2,3},{3,2},{4,5},{5,4},{6,7},{7,6},{8,9},{9,8},{10,11... | collective-permute-start | bytes 12582920 | tf_op jit(solution)/shard_map/ppermute | solution.py:349
  3.7 7.7 %solve_lower.1 = (f32[128,512]{1,0:T(8,128)}, f32[128,512]{1,0:T(8,128)}, f32[1,512]{1,0:T(1,128)}, f32[1,512]{1,0:T(1,128)}) custom-call(s32[32]{0:T(128)} %slots.5, s32[1]{0:T(128)} %bitcast.me, f32[512,512]{1,0:T(8,128)} %s_ref.5, f32[512,512]{1,0:T(8,128)} %t_ref.5, f32[512,512]{1,0:T(8,128)} %r_ref.5, f32[32,128]{1,0:T(8,128)} %bitcast.11, ...), custom_call_target="tpu_custom_call" | custom-call | flops 1000 | bytes 1000 | tf_op jit(solution)/shard_map/solve_lower/pallas_call | solution.py:146
  11.4 0.0 collective-permute-start
  11.4 1.4 %fusion = (s32[1]{0:T(128)}, s32[1]{0:T(128)}) fusion(s32[32]{0:T(128)} %slots.5), kind=kLoop, calls=%fused_computation.11 | loop fusion | bytes 16 | tf_op jit(solution)/shard_map/slice | solution.py:343
  14.7 0.0 collective-permute-done
  14.7 0.0 copy-start.9
  14.7 0.7 copy-done.9
  15.4 0.0 copy-start
  15.4 0.0 copy-start.1
  15.4 0.0 copy-start.2
  15.4 0.0 copy-start.5
  15.4 0.0 copy-start.6
  15.4 0.0 copy-start.7
  15.4 1.1 %broadcast_select_fusion.1 = f32[128,512]{1,0:T(8,128)S(1)} fusion(f32[128,512]{1,0:T(8,128)} %get-tuple-element.13, f32[128,512]{1,0:T(8,128)} %copy-done.9, pred[]{:T(512)S(6)} %eq.13), kind=kLoop, calls=%fused_computation.3 | loop fusion | flops 65536 | bytes 786433 | tf_op jit(solution)/shard_map/jit(_where)/select_n | solution.py:312
  16.6 1.6 %collective-permute-start.1 = (f32[64,512]{1,0:T(8,128)S(1)}, f32[64,512]{1,0:T(8,128)}, u32[]{:S(2)}, u32[]{:S(2)}) collective-permute-start(f32[64,512]{1,0:T(8,128)S(1)} %slice_select_fusion.1), channel_id=1, source_target_pairs={{0,4},{2,6},{4,0},{6,2},{8,12},{10,14},{12,8},{14,10},{16,20},{18,... | collective-permute-start | bytes 393224 | tf_op jit(solution)/shard_map/ppermute | solution.py:309
  18.2 4.5 %collective-permute-done.1 = f32[64,512]{1,0:T(8,128)} collective-permute-done((f32[64,512]{1,0:T(8,128)S(1)}, f32[64,512]{1,0:T(8,128)}, u32[]{:S(2)}, u32[]{:S(2)}) %collective-permute-start.1) | collective-permute-done | bytes 131104 | tf_op jit(solution)/shard_map/ppermute | solution.py:309
  22.7 0.9 select_select_fusion.1
  23.6 1.6 %collective-permute-start.2 = (f32[64,512]{1,0:T(8,128)S(1)}, f32[64,512]{1,0:T(8,128)S(1)}, u32[]{:S(2)}, u32[]{:S(2)}) collective-permute-start(f32[64,512]{1,0:T(8,128)S(1)} %select_select_fusion.1), channel_id=1, source_target_pairs={{0,8},{2,10},{4,12},{6,14},{8,0},{10,2},{12,4},{14,6},{16,24},{18,... | collective-permute-start | bytes 393224 | tf_op jit(solution)/shard_map/ppermute | solution.py:309
  25.3 3.5 %collective-permute-done.2 = f32[64,512]{1,0:T(8,128)S(1)} collective-permute-done((f32[64,512]{1,0:T(8,128)S(1)}, f32[64,512]{1,0:T(8,128)S(1)}, u32[]{:S(2)}, u32[]{:S(2)}) %collective-permute-start.2) | collective-permute-done | bytes 131104 | tf_op jit(solution)/shard_map/ppermute | solution.py:309
  28.8 2.7 %collective-permute-start.3 = (f32[64,512]{1,0:T(8,128)S(1)}, f32[64,512]{1,0:T(8,128)S(1)}, u32[]{:S(2)}, u32[]{:S(2)}) collective-permute-start(f32[64,512]{1,0:T(8,128)S(1)} %broadcast_select_fusion.4), channel_id=1, source_target_pairs={{0,16},{2,18},{4,20},{6,22},{8,24},{10,26},{12,28},{14,30},{16,0},... | collective-permute-start | bytes 393224 | tf_op jit(solution)/shard_map/ppermute | solution.py:309
  31.5 5.5 %collective-permute-done.3 = f32[64,512]{1,0:T(8,128)S(1)} collective-permute-done((f32[64,512]{1,0:T(8,128)S(1)}, f32[64,512]{1,0:T(8,128)S(1)}, u32[]{:S(2)}, u32[]{:S(2)}) %collective-permute-start.3) | collective-permute-done | bytes 131104 | tf_op jit(solution)/shard_map/ppermute | solution.py:309
  37.0 0.0 copy-start.8
  37.0 0.1 collective-permute-start.6
  37.1 1.6 %collective-permute-start.5 = (f32[64,512]{1,0:T(8,128)S(1)}, f32[64,512]{1,0:T(8,128)S(1)}, u32[]{:S(2)}, u32[]{:S(2)}) collective-permute-start(f32[64,512]{1,0:T(8,128)S(1)} %broadcast_select_fusion.5.refs_0_), channel_id=1, source_target_pairs={{0,2},{2,0},{4,6},{6,4},{8,10},{10,8},{12,14},{14,12},{16,18},{18,... | collective-permute-start | bytes 393224 | tf_op jit(solution)/shard_map/ppermute | solution.py:309
  38.7 0.5 collective-permute-start.4
  39.2 3.6 %collective-permute-done.6.refs_3_ = f32[64,512]{1,0:T(8,128)S(1)} collective-permute-done((f32[64,512]{1,0:T(8,128)S(1)}, f32[64,512]{1,0:T(8,128)S(1)}, u32[]{:S(2)}, u32[]{:S(2)}) %collective-permute-start.6) | collective-permute-done | bytes 131104 | tf_op jit(solution)/shard_map/ppermute | solution.py:309
  42.8 0.0 collective-permute-done.5.refs_2_
  42.8 2.8 %collective-permute-done.4.refs_1_ = f32[64,512]{1,0:T(8,128)S(1)} collective-permute-done((f32[64,512]{1,0:T(8,128)S(1)}, f32[64,512]{1,0:T(8,128)S(1)}, u32[]{:S(2)}, u32[]{:S(2)}) %collective-permute-start.4) | collective-permute-done | bytes 131104 | tf_op jit(solution)/shard_map/ppermute | solution.py:309
  45.7 0.0 copy-done.8
  45.7 0.0 copy-done.11
  45.7 0.0 copy-done.12
  45.7 0.6 copy-done.13
  46.3 8.6 %solve_upper.1 = (f32[128,512]{1,0:T(8,128)}, f32[128,512]{1,0:T(8,128)}, f32[256,512]{1,0:T(8,128)}) custom-call(s32[32]{0:T(128)} %slots.5, s32[1]{0:T(128)} %bitcast.me, f32[512,512]{1,0:T(8,128)} %s_ref.5, f32[512,512]{1,0:T(8,128)} %t_ref.5, f32[512,512]{1,0:T(8,128)} %r_ref.5, f32[1,512]{1,0:T(1,128)} %get-tuple-element.11.alpha_ref, ...), custom_call_target="tpu_custom_call" | custom-call | flops 1000 | bytes 1000 | tf_op jit(solution)/shard_map/solve_upper/pallas_call | solution.py:182
  54.9 0.2 collective-permute-start.7
  57.2 0.0 collective-permute-done.7
  57.2 0.0 copy-start.10
  57.2 0.7 copy-done.10
  57.9 1.0 broadcast_select_fusion
  58.9 0.7 collective-permute-start.8
  59.6 5.2 %collective-permute-done.8 = f32[64,512]{1,0:T(8,128)} collective-permute-done((f32[64,512]{1,0:T(8,128)S(1)}, f32[64,512]{1,0:T(8,128)}, u32[]{:S(2)}, u32[]{:S(2)}) %collective-permute-start.8) | collective-permute-done | bytes 131104 | tf_op jit(solution)/shard_map/ppermute | solution.py:309
  64.8 0.9 select_select_fusion
  65.8 0.1 collective-permute-start.9
  65.9 4.9 %collective-permute-done.9 = f32[64,512]{1,0:T(8,128)S(1)} collective-permute-done((f32[64,512]{1,0:T(8,128)S(1)}, f32[64,512]{1,0:T(8,128)S(1)}, u32[]{:S(2)}, u32[]{:S(2)}) %collective-permute-start.9) | collective-permute-done | bytes 131104 | tf_op jit(solution)/shard_map/ppermute | solution.py:309
  70.8 1.3 %collective-permute-start.10 = (f32[64,512]{1,0:T(8,128)S(1)}, f32[64,512]{1,0:T(8,128)S(1)}, u32[]{:S(2)}, u32[]{:S(2)}) collective-permute-start(f32[64,512]{1,0:T(8,128)S(1)} %broadcast_select_fusion.2), channel_id=1, source_target_pairs={{0,16},{2,18},{4,20},{6,22},{8,24},{10,26},{12,28},{14,30},{16,0},... | collective-permute-start | bytes 393224 | tf_op jit(solution)/shard_map/ppermute | solution.py:309
  72.1 6.6 %collective-permute-done.10 = f32[64,512]{1,0:T(8,128)S(1)} collective-permute-done((f32[64,512]{1,0:T(8,128)S(1)}, f32[64,512]{1,0:T(8,128)S(1)}, u32[]{:S(2)}, u32[]{:S(2)}) %collective-permute-start.10) | collective-permute-done | bytes 131104 | tf_op jit(solution)/shard_map/ppermute | solution.py:309
  78.7 0.1 collective-permute-start.13
  78.8 0.1 collective-permute-start.12
  78.9 2.0 %collective-permute-start.11 = (f32[64,512]{1,0:T(8,128)S(1)}, f32[64,512]{1,0:T(8,128)}, u32[]{:S(2)}, u32[]{:S(2)}) collective-permute-start(f32[64,512]{1,0:T(8,128)S(1)} %broadcast_select_fusion.3.refs_0_), channel_id=1, source_target_pairs={{0,4},{2,6},{4,0},{6,2},{8,12},{10,14},{12,8},{14,10},{16,20},{18,... | collective-permute-start | bytes 393224 | tf_op jit(solution)/shard_map/ppermute | solution.py:309
  81.0 0.1 pad_add_fusion.parts
  81.0 3.5 %collective-permute-done.13.refs_3_ = f32[64,512]{1,0:T(8,128)S(1)} collective-permute-done((f32[64,512]{1,0:T(8,128)S(1)}, f32[64,512]{1,0:T(8,128)S(1)}, u32[]{:S(2)}, u32[]{:S(2)}) %collective-permute-start.13) | collective-permute-done | bytes 131104 | tf_op jit(solution)/shard_map/ppermute | solution.py:309
  84.5 0.0 collective-permute-done.12.refs_2_
  84.5 2.0 %collective-permute-done.11.refs_1_ = f32[64,512]{1,0:T(8,128)} collective-permute-done((f32[64,512]{1,0:T(8,128)S(1)}, f32[64,512]{1,0:T(8,128)}, u32[]{:S(2)}, u32[]{:S(2)}) %collective-permute-start.11) | collective-permute-done | bytes 131104 | tf_op jit(solution)/shard_map/ppermute | solution.py:309
  86.6 0.0 copy-done
  86.6 0.0 copy-done.1
  86.6 0.0 copy-done.2
  86.6 0.0 copy-done.5
  86.6 0.0 copy-done.6
  86.6 0.0 copy-done.7
  86.6 0.0 copy-start.4
  86.6 1.0 copy-done.4
  87.7 4.3 %finish_sides.1 = (f32[512,512]{1,0:T(8,128)}, bf16[1536,512]{1,0:T(8,128)(2,1)S(1)}) custom-call(s32[32]{0:T(128)S(1)} %copy-done.5, s32[1]{0:T(128)} %bitcast.me, s32[2]{0:T(128)S(1)} %pad_add_fusion.parts, f32[512,512]{1,0:T(8,128)S(1)} %copy-done, f32[512,512]{1,0:T(8,128)S(1)} %copy-done.1, f32[512,512]{1,0:T(8,128)S(1)} %copy-done.2, ...), custom_call_target="tpu_custom_call" | custom-call | flops 1000 | bytes 1000 | tf_op jit(solution)/shard_map/finish_sides/pallas_call | solution.py:245
  92.0 2.6 %collective-permute-done.14.refs_1_ = f32[8192,128]{1,0:T(8,128)} collective-permute-done((f32[8192,128]{1,0:T(8,128)}, f32[8192,128]{1,0:T(8,128)}, u32[]{:S(2)}, u32[]{:S(2)}) %collective-permute-start.14) | collective-permute-done | bytes 4194336 | tf_op jit(solution)/shard_map/ppermute | solution.py:349
  94.6 0.0 copy-done.3
  94.6 11.4 %add_product.1 = f32[4096,512]{1,0:T(8,128)} custom-call(f32[4096,512]{1,0:T(8,128)} %base_ref.1, bf16[1536,512]{1,0:T(8,128)(2,1)S(1)} %get-tuple-element.19.terms_ref, f32[8192,128]{1,0:T(8,128)S(1)} %bitcast.10, f32[8192,128]{1,0:T(8,128)} %collective-permute-done.14.refs_1_), custom_call_target="tpu_custom_call" | custom-call | flops 1000 | bytes 1000 | tf_op jit(solution)/shard_map/add_product/pallas_call | solution.py:282
  (10 shorter events, 0.1 us)
Async XLA Ops:
  0.6 93.9 %collective-permute-start.14 = (f32[8192,128]{1,0:T(8,128)}, f32[8192,128]{1,0:T(8,128)}, u32[]{:S(2)}, u32[]{:S(2)}) collective-permute-start(f32[8192,128]{1,0:T(8,128)} %bitcast.9), channel_id=1, source_target_pairs={{0,1},{1,0},{2,3},{3,2},{4,5},{5,4},{6,7},{7,6},{8,9},{9,8},{10,11... | collective-permute-start | bytes 12582920 | tf_op jit(solution)/shard_map/ppermute | solution.py:349
  11.4 3.3 %collective-permute-start = (f32[128,512]{1,0:T(8,128)}, f32[128,512]{1,0:T(8,128)S(1)}, u32[]{:S(2)}, u32[]{:S(2)}) collective-permute-start(f32[128,512]{1,0:T(8,128)} %get-tuple-element.14), channel_id=1, source_target_pairs={{0,2},{2,0},{4,6},{6,4},{8,10},{10,8},{12,14},{14,12},{16,18},{18,... | collective-permute-start | bytes 786440 | tf_op jit(solution)/shard_map/ppermute | solution.py:309
  14.7 0.7 copy-start.9
  15.4 71.2 %copy-start = (f32[512,512]{1,0:T(8,128)S(1)}, f32[512,512]{1,0:T(8,128)}, u32[]{:S(2)}) copy-start(f32[512,512]{1,0:T(8,128)} %r_ref.5) | copy-start | bytes 3145732
  15.4 71.2 %copy-start.1 = (f32[512,512]{1,0:T(8,128)S(1)}, f32[512,512]{1,0:T(8,128)}, u32[]{:S(2)}) copy-start(f32[512,512]{1,0:T(8,128)} %s_ref.5) | copy-start | bytes 3145732
  15.4 71.2 %copy-start.2 = (f32[512,512]{1,0:T(8,128)S(1)}, f32[512,512]{1,0:T(8,128)}, u32[]{:S(2)}) copy-start(f32[512,512]{1,0:T(8,128)} %t_ref.5) | copy-start | bytes 3145732
  15.4 71.2 %copy-start.5 = (s32[32]{0:T(128)S(1)}, s32[32]{0:T(128)}, u32[]{:S(2)}) copy-start(s32[32]{0:T(128)} %slots.5) | copy-start | bytes 388
  15.4 71.2 %copy-start.6 = (f32[1,512]{1,0:T(1,128)S(1)}, f32[1,512]{1,0:T(1,128)}, u32[]{:S(2)}) copy-start(f32[1,512]{1,0:T(1,128)} %get-tuple-element.11.alpha_ref) | copy-start | bytes 6148
  15.4 71.2 %copy-start.7 = (f32[1,512]{1,0:T(1,128)S(1)}, f32[1,512]{1,0:T(1,128)}, u32[]{:S(2)}) copy-start(f32[1,512]{1,0:T(1,128)} %get-tuple-element.12.beta_ref) | copy-start | bytes 6148
  16.6 6.1 %collective-permute-start.1 = (f32[64,512]{1,0:T(8,128)S(1)}, f32[64,512]{1,0:T(8,128)}, u32[]{:S(2)}, u32[]{:S(2)}) collective-permute-start(f32[64,512]{1,0:T(8,128)S(1)} %slice_select_fusion.1), channel_id=1, source_target_pairs={{0,4},{2,6},{4,0},{6,2},{8,12},{10,14},{12,8},{14,10},{16,20},{18,... | collective-permute-start | bytes 393224 | tf_op jit(solution)/shard_map/ppermute | solution.py:309
  23.6 5.2 %collective-permute-start.2 = (f32[64,512]{1,0:T(8,128)S(1)}, f32[64,512]{1,0:T(8,128)S(1)}, u32[]{:S(2)}, u32[]{:S(2)}) collective-permute-start(f32[64,512]{1,0:T(8,128)S(1)} %select_select_fusion.1), channel_id=1, source_target_pairs={{0,8},{2,10},{4,12},{6,14},{8,0},{10,2},{12,4},{14,6},{16,24},{18,... | collective-permute-start | bytes 393224 | tf_op jit(solution)/shard_map/ppermute | solution.py:309
  28.8 8.1 %collective-permute-start.3 = (f32[64,512]{1,0:T(8,128)S(1)}, f32[64,512]{1,0:T(8,128)S(1)}, u32[]{:S(2)}, u32[]{:S(2)}) collective-permute-start(f32[64,512]{1,0:T(8,128)S(1)} %broadcast_select_fusion.4), channel_id=1, source_target_pairs={{0,16},{2,18},{4,20},{6,22},{8,24},{10,26},{12,28},{14,30},{16,0},... | collective-permute-start | bytes 393224 | tf_op jit(solution)/shard_map/ppermute | solution.py:309
  37.0 8.7 %copy-start.8 = (f32[64,512]{1,0:T(8,128)}, f32[64,512]{1,0:T(8,128)S(1)}, u32[]{:S(2)}) copy-start(f32[64,512]{1,0:T(8,128)S(1)} %broadcast_select_fusion.5.refs_0_) | copy-start | bytes 393220
  37.0 5.8 %collective-permute-start.6 = (f32[64,512]{1,0:T(8,128)S(1)}, f32[64,512]{1,0:T(8,128)S(1)}, u32[]{:S(2)}, u32[]{:S(2)}) collective-permute-start(f32[64,512]{1,0:T(8,128)S(1)} %broadcast_select_fusion.5.refs_0_), channel_id=1, source_target_pairs={{0,6},{2,4},{4,2},{6,0},{8,14},{10,12},{12,10},{14,8},{16,22},{18,... | collective-permute-start | bytes 393224 | tf_op jit(solution)/shard_map/ppermute | solution.py:309
  37.1 5.7 %collective-permute-start.5 = (f32[64,512]{1,0:T(8,128)S(1)}, f32[64,512]{1,0:T(8,128)S(1)}, u32[]{:S(2)}, u32[]{:S(2)}) collective-permute-start(f32[64,512]{1,0:T(8,128)S(1)} %broadcast_select_fusion.5.refs_0_), channel_id=1, source_target_pairs={{0,2},{2,0},{4,6},{6,4},{8,10},{10,8},{12,14},{14,12},{16,18},{18,... | collective-permute-start | bytes 393224 | tf_op jit(solution)/shard_map/ppermute | solution.py:309
  38.7 7.0 %collective-permute-start.4 = (f32[64,512]{1,0:T(8,128)S(1)}, f32[64,512]{1,0:T(8,128)S(1)}, u32[]{:S(2)}, u32[]{:S(2)}) collective-permute-start(f32[64,512]{1,0:T(8,128)S(1)} %broadcast_select_fusion.5.refs_0_), channel_id=1, source_target_pairs={{0,4},{2,6},{4,0},{6,2},{8,12},{10,14},{12,8},{14,10},{16,20},{18,... | collective-permute-start | bytes 393224 | tf_op jit(solution)/shard_map/ppermute | solution.py:309
  42.8 2.9 %copy-start.11 = (f32[64,512]{1,0:T(8,128)}, f32[64,512]{1,0:T(8,128)S(1)}, u32[]{:S(2)}) copy-start(f32[64,512]{1,0:T(8,128)S(1)} %collective-permute-done.6.refs_3_) | copy-start | bytes 393220
  42.8 2.9 %copy-start.12 = (f32[64,512]{1,0:T(8,128)}, f32[64,512]{1,0:T(8,128)S(1)}, u32[]{:S(2)}) copy-start(f32[64,512]{1,0:T(8,128)S(1)} %collective-permute-done.5.refs_2_) | copy-start | bytes 393220
  45.7 0.7 copy-start.13
  54.9 2.3 %collective-permute-start.7 = (f32[128,512]{1,0:T(8,128)}, f32[128,512]{1,0:T(8,128)S(1)}, u32[]{:S(2)}, u32[]{:S(2)}) collective-permute-start(f32[128,512]{1,0:T(8,128)} %get-tuple-element.17), channel_id=1, source_target_pairs={{0,2},{2,0},{4,6},{6,4},{8,10},{10,8},{12,14},{14,12},{16,18},{18,... | collective-permute-start | bytes 786440 | tf_op jit(solution)/shard_map/ppermute | solution.py:309
  57.2 0.7 copy-start.10
  58.9 5.9 %collective-permute-start.8 = (f32[64,512]{1,0:T(8,128)S(1)}, f32[64,512]{1,0:T(8,128)}, u32[]{:S(2)}, u32[]{:S(2)}) collective-permute-start(f32[64,512]{1,0:T(8,128)S(1)} %slice_select_fusion), channel_id=1, source_target_pairs={{0,4},{2,6},{4,0},{6,2},{8,12},{10,14},{12,8},{14,10},{16,20},{18,... | collective-permute-start | bytes 393224 | tf_op jit(solution)/shard_map/ppermute | solution.py:309
  65.8 5.0 %collective-permute-start.9 = (f32[64,512]{1,0:T(8,128)S(1)}, f32[64,512]{1,0:T(8,128)S(1)}, u32[]{:S(2)}, u32[]{:S(2)}) collective-permute-start(f32[64,512]{1,0:T(8,128)S(1)} %select_select_fusion), channel_id=1, source_target_pairs={{0,8},{2,10},{4,12},{6,14},{8,0},{10,2},{12,4},{14,6},{16,24},{18,... | collective-permute-start | bytes 393224 | tf_op jit(solution)/shard_map/ppermute | solution.py:309
  70.8 7.9 %collective-permute-start.10 = (f32[64,512]{1,0:T(8,128)S(1)}, f32[64,512]{1,0:T(8,128)S(1)}, u32[]{:S(2)}, u32[]{:S(2)}) collective-permute-start(f32[64,512]{1,0:T(8,128)S(1)} %broadcast_select_fusion.2), channel_id=1, source_target_pairs={{0,16},{2,18},{4,20},{6,22},{8,24},{10,26},{12,28},{14,30},{16,0},... | collective-permute-start | bytes 393224 | tf_op jit(solution)/shard_map/ppermute | solution.py:309
  78.7 5.8 %collective-permute-start.13 = (f32[64,512]{1,0:T(8,128)S(1)}, f32[64,512]{1,0:T(8,128)S(1)}, u32[]{:S(2)}, u32[]{:S(2)}) collective-permute-start(f32[64,512]{1,0:T(8,128)S(1)} %broadcast_select_fusion.3.refs_0_), channel_id=1, source_target_pairs={{0,6},{2,4},{4,2},{6,0},{8,14},{10,12},{12,10},{14,8},{16,22},{18,... | collective-permute-start | bytes 393224 | tf_op jit(solution)/shard_map/ppermute | solution.py:309
  78.8 5.7 %collective-permute-start.12 = (f32[64,512]{1,0:T(8,128)S(1)}, f32[64,512]{1,0:T(8,128)S(1)}, u32[]{:S(2)}, u32[]{:S(2)}) collective-permute-start(f32[64,512]{1,0:T(8,128)S(1)} %broadcast_select_fusion.3.refs_0_), channel_id=1, source_target_pairs={{0,2},{2,0},{4,6},{6,4},{8,10},{10,8},{12,14},{14,12},{16,18},{18,... | collective-permute-start | bytes 393224 | tf_op jit(solution)/shard_map/ppermute | solution.py:309
  78.9 7.7 %collective-permute-start.11 = (f32[64,512]{1,0:T(8,128)S(1)}, f32[64,512]{1,0:T(8,128)}, u32[]{:S(2)}, u32[]{:S(2)}) collective-permute-start(f32[64,512]{1,0:T(8,128)S(1)} %broadcast_select_fusion.3.refs_0_), channel_id=1, source_target_pairs={{0,4},{2,6},{4,0},{6,2},{8,12},{10,14},{12,8},{14,10},{16,20},{18,... | collective-permute-start | bytes 393224 | tf_op jit(solution)/shard_map/ppermute | solution.py:309
  81.0 13.6 %copy-start.3 = (f32[4096,2,128]{2,1,0:T(2,128)S(1)}, f32[4096,2,128]{2,1,0:T(2,128)}, u32[]{:S(2)}) copy-start(f32[4096,2,128]{2,1,0:T(2,128)} %param.16) | copy-start | bytes 12582916
  86.6 1.0 copy-start.4
